TPU v7x, 32 devices: a whole 2x2x4 slice. The times are simulated.
32 devices in a mesh: fsdp: 16 (over z, x, core), tensor: 2 (over y).
Axes of the slice: x: 2, y: 2, z: 4, core: 2. Of those that a mesh axis runs over, the one named last changes fastest.
Arguments:
- gate_pre: bfloat16 [3072, 14336], P(('fsdp', 'tensor')), may hold values from -6 to 6
- up_pre: bfloat16 [3072, 14336], P(('fsdp', 'tensor')), may hold values from -6 to 6
- cotangent: bfloat16 [3072, 4096], P('fsdp'), may hold values from -6 to 6
- w_slots: bfloat16 [2, 48, 128, 128], P('tensor', 'fsdp'), may hold values from -0.15625 to 0.15625
- slot_ids: int32 [2, 48], P('tensor'), may hold values from -1 to 1791, as said below
Outputs:
- d_gate: bfloat16 [3072, 14336], P(('fsdp', 'tensor'))
- d_up: bfloat16 [3072, 14336], P(('fsdp', 'tensor'))
- w_grad: float32 [2, 48, 128, 128], P('tensor', 'fsdp')
Inputs may be any that keep to these rules, and one draw needn't show every extreme that they name: `slot_ids`: in row t, slots s * 3 to s * 3 + 2 list the kept blocks owned by fsdp index s in tensor slice t as local row block * 32 + column block, filling the first slots and -1 in the rest; every owner has 2 or 3 kept blocks, some owner of every row exactly 3 and some exactly 2; no block id appears twice in a row.
All inputs are finite; a program needn't handle non-finite values.
Results may differ from a plain program's by a relative error of at most 0.0085.
Values may be sent and summed in bfloat16 or wider, within the bound.
A program may use at most 128 MiB of HBM per device.

v0:
```python
import math

import jax
import jax.numpy as jnp
from jax import lax
from jax.sharding import PartitionSpec as P


def swiglu_value(gate_part, up_part):
    gate_f = gate_part.astype(jnp.float32)
    gate_sig = jax.nn.sigmoid(gate_f)
    return (gate_f * gate_sig * up_part.astype(jnp.float32)).astype(jnp.bfloat16)


def swiglu_grads(dh_part, gate_part, up_part):
    gate_f = gate_part.astype(jnp.float32)
    up_f = up_part.astype(jnp.float32)
    gate_sig = jax.nn.sigmoid(gate_f)
    dh_f = dh_part.astype(jnp.float32)
    grad_gate = (dh_f * up_f * (gate_sig * (1.0 + gate_f * (1.0 - gate_sig)))).astype(jnp.bfloat16)
    grad_up = (dh_f * (gate_f * gate_sig)).astype(jnp.bfloat16)
    return (grad_gate, grad_up)


def body(gate_pre, up_pre, cotangent, w_slots, slot_ids):
    n_fsdp = lax.axis_size("fsdp")
    block_size = w_slots.shape[2]
    token_count = cotangent.shape[0]
    model_width = cotangent.shape[1]
    col_count = model_width // block_size
    ff_dev = gate_pre.shape[1] // lax.axis_size("tensor")
    row_count = ff_dev // block_size
    slot_total = slot_ids.shape[1]
    cap_local = w_slots.shape[1]
    slot_list = slot_ids[0]
    usable = slot_list >= 0
    safe_ids = jnp.maximum(slot_list, 0)
    row_index = jnp.where(usable, safe_ids // col_count, row_count)
    col_index = safe_ids % col_count
    row_clip = jnp.minimum(row_index, row_count - 1)
    usable_f = usable.astype(jnp.float32)
    row_range = jnp.arange(row_count, dtype=jnp.int32)
    dy_blocks = cotangent.reshape(token_count, col_count, block_size)
    hidden_seq = swiglu_value(gate_pre, up_pre)
    hidden = lax.all_to_all(hidden_seq, "tensor", split_axis=1, concat_axis=0, tiled=True)
    start_sum = jnp.zeros((token_count, row_count, block_size), jnp.float32)
    running = start_sum
    shard_piece = lax.all_gather(w_slots, "fsdp", axis=1, tiled=True)
    slot_count = shard_piece.shape[1]
    sub_size = math.gcd(slot_count, 48)
    rows_part = row_index.reshape(slot_count // sub_size, sub_size)
    cols_part = col_index.reshape(slot_count // sub_size, sub_size)
    weight_part = shard_piece[0].reshape(slot_count // sub_size, sub_size, block_size, block_size)

    def advance(carried, packed_item):
        rows_now, cols_now, weight_now = packed_item
        dy_picked = jnp.take(dy_blocks, cols_now, axis=1)
        contrib = jnp.einsum(
            "tsb,sab->tsa", dy_picked, weight_now, preferred_element_type=jnp.float32
        )
        onehot = (rows_now[:, None] == row_range[None, :]).astype(jnp.float32)
        added = jnp.einsum("tsa,sr->tra", contrib, onehot, precision=lax.Precision.HIGHEST)
        return (carried + added, None)

    running, _ = lax.scan(advance, running, (rows_part, cols_part, weight_part))
    d_hidden = running.reshape(token_count, ff_dev).astype(jnp.bfloat16)
    grad_scale = 1.0 / math.sqrt(token_count * n_fsdp)
    hidden_blocks = hidden.reshape(token_count, row_count, block_size)
    group_size = math.gcd(slot_total, 48)
    group_count = slot_total // group_size

    def partial_group(packed_item):
        rows_now, cols_now, scale_now = packed_item
        h_picked = jnp.take(hidden_blocks, rows_now, axis=1)
        dy_picked = jnp.take(dy_blocks, cols_now, axis=1)
        product = jnp.einsum(
            "tsa,tsb->sab", h_picked, dy_picked, preferred_element_type=jnp.float32
        )
        return (product * scale_now[:, None, None]).astype(jnp.bfloat16)

    partials = lax.map(
        partial_group,
        (
            row_clip.reshape(group_count, group_size),
            col_index.reshape(group_count, group_size),
            (grad_scale * usable_f).reshape(group_count, group_size),
        ),
    )
    partials = partials.reshape(slot_total, block_size, block_size)
    arrived = lax.all_to_all(partials, "fsdp", split_axis=0, concat_axis=0, tiled=True)
    w_grad = (
        arrived.astype(jnp.float32)
        .reshape(n_fsdp, cap_local, block_size, block_size)
        .sum(axis=0)[None]
    )
    dh_seq = lax.all_to_all(d_hidden, "tensor", split_axis=0, concat_axis=1, tiled=True)
    d_gate, d_up = swiglu_grads(dh_seq, gate_pre, up_pre)
    return (d_gate, d_up, w_grad)


def solution(mesh):
    placed = (
        P(("fsdp", "tensor"), None),
        P(("fsdp", "tensor"), None),
        P("fsdp", None),
        P("tensor", "fsdp", None, None),
        P("tensor", None),
    )
    return jax.shard_map(
        body,
        mesh=mesh,
        in_specs=placed,
        out_specs=(
            P(("fsdp", "tensor"), None),
            P(("fsdp", "tensor"), None),
            P("tensor", "fsdp", None, None),
        ),
        check_vma=False,
    )
```

profile of v0, /device:TPU:0, one launch (start us, length us, event | category | flops | bytes accessed | tf_op | source)
XLA Modules:
  0.0 212.5 jit_solution(13662757047801409975)
XLA Ops:
  7.2 0.0 all-gather.2.cloned.1.call-start
  7.2 0.7 all-gather.2.cloned.1.call-update
  7.9 0.7 compare_and_fusion.1
  8.6 0.4 copy_bitcast_fusion.1
  9.0 2.3 %gather_fusion.1 = bf16[48,192,128]{2,1,0:T(8,128)(2,1)} fusion(bf16[192,32,128]{2,0,1:T(8,128)(2,1)S(1)} %copy_bitcast_fusion.1, s32[1024]{0:T(1024)S(1)} %pad_clamp_fusion.1), kind=kCustom, calls=%fused_computation.clone | custom fusion | bytes 4718784 | tf_op jit(solution)/shard_map/while/body/eval_jaxpr/jit(_take)/gather | solution.py:57
  11.4 41.3 %all-gather.2.cloned.1.call-done = bf16[1,48,128,128]{3,2,0,1:T(8,128)(2,1)} async-done(((bf16[1,3,128,128]{3,2,0,1:T(8,128)(2,1)}), bf16[1,48,128,128]{3,2,0,1:T(8,128)(2,1)}) %all-gather.2.cloned.1.call-update) | async-done | bytes 1572880 | tf_op jit(solution)/shard_map/all_gather | solution.py:48
  52.7 3.3 %fusion.17 = f32[192,48,128]{2,0,1:T(8,128)S(1)} fusion(bf16[1,48,128,128]{3,2,0,1:T(8,128)(2,1)} %all-gather.2.cloned.1.call-done, bf16[48,192,128]{2,1,0:T(8,128)(2,1)} %gather_fusion.1, pred[48]{0:T(512)(128)(4,1)S(1)} %get-tuple-element.46), kind=kOutput, calls=%fused_computation.31 | convolution fusion | flops 303169536 | bytes 8650800 | tf_op jit(solution)/shard_map/while/body/eval_jaxpr/tsb,sab->tsa/dot_general | solution.py:58
  56.0 8.3 %convert_bitcast_fusion.1 = bf16[192,56,128]{2,1,0:T(8,128)(2,1)} fusion(f32[192,48,128]{2,0,1:T(8,128)S(1)} %fusion.17, s32[48]{0:T(128)S(1)} %get-tuple-element.33), kind=kOutput, calls=%fused_computation.22 | convolution fusion | flops 794102400 | bytes 7471296 | tf_op jit(solution)/shard_map/while/body/eval_jaxpr/tsa,sr->tra/dot_general | solution.py:62
  64.3 5.3 %convert_element_type.46 = bf16[2,96,7168]{2,1,0:T(8,128)(2,1)} reshape(bf16[192,56,128]{2,1,0:T(8,128)(2,1)} %convert_bitcast_fusion.1) | data formatting | bytes 5505024 | tf_op jit(solution)/shard_map/convert_element_type | solution.py:66
  69.5 36.4 %all_to_all.31 = bf16[2,96,7168]{2,1,0:T(8,128)(2,1)S(1)} all-to-all(bf16[2,96,7168]{2,1,0:T(8,128)(2,1)} %convert_element_type.46), channel_id=1, replica_groups=mesh['fsdp'=16,'tensor'=2] {'tensor'}, dimensions={0} | all-to-all | bytes 5505024 | tf_op jit(solution)/shard_map/all_to_all | solution.py:96
  106.0 0.6 convert_bitcast_fusion
  106.6 0.5 copy.25
  107.1 1.2 copy-done.1
  108.4 0.8 copy-done.2
  109.2 4.7 %multiply_convert_fusion = (bf16[96,14336]{1,0:T(8,128)(2,1)}, bf16[96,14336]{1,0:T(8,128)(2,1)}, bf16[96,14336]{1,0:T(8,128)(2,1)S(1)}) fusion(f32[96,14336]{1,0:T(8,128)S(1)} %bitcast.90, bf16[96,14336]{1,0:T(8,128)(2,1)S(1)} %copy-done.1, bf16[96,14336]{1,0:T(8,128)(2,1)S(1)} %copy-done.2), kind=kLoop, calls=%fused_computation.16 | loop fusion | flops 23396352 | bytes 19267584 | tf_op jit(solution)/shard_map/convert_element_type | solution.py:21
  113.9 1.8 copy.33
  115.7 5.2 %all-to-all-start.1 = ((bf16[96,2,7168]{2,0,1:T(8,128)(2,1)}), bf16[96,2,7168]{2,0,1:T(8,128)(2,1)}, u32[]{:S(2)}, u32[]{:S(2)}) async-start(bf16[96,2,7168]{2,0,1:T(8,128)(2,1)} %bitcast.92), calls=%async_computation.1 | async-start | bytes 5505024 | tf_op jit(solution)/shard_map/all_to_all | solution.py:45
  121.0 31.8 %all-to-all-done.1 = bf16[96,2,7168]{2,0,1:T(8,128)(2,1)} async-done(((bf16[96,2,7168]{2,0,1:T(8,128)(2,1)}), bf16[96,2,7168]{2,0,1:T(8,128)(2,1)}, u32[]{:S(2)}, u32[]{:S(2)}) %all-to-all-start.1) | async-done | bytes 2752544 | tf_op jit(solution)/shard_map/all_to_all | solution.py:45
  152.8 2.3 %copy.26 = bf16[24,8,56,128]{3,2,1,0:T(8,128)(2,1)S(1)} copy(bf16[24,8,56,128]{3,1,2,0:T(8,128)(2,1)} %bitcast.27) | data formatting | bytes 5505024
  155.1 2.2 %copy.22 = bf16[192,56,128]{2,0,1:T(8,128)(2,1)} copy(bf16[192,56,128]{2,1,0:T(8,128)(2,1)S(1)} %bitcast.93) | data formatting | bytes 5505024 | tf_op jit(solution)/shard_map/reshape | solution.py:68
  157.3 4.1 %gather_fusion = bf16[48,192,128]{2,1,0:T(8,128)(2,1)} fusion(bf16[192,56,128]{2,0,1:T(8,128)(2,1)} %copy.22, s32[1024]{0:T(1024)S(1)} %pad_clamp_fusion), kind=kCustom, calls=%fused_computation.1 | custom fusion | bytes 4718784 | tf_op jit(solution)/shard_map/while/body/eval_jaxpr/jit(_take)/gather | solution.py:74
  161.4 3.8 %multiply_convert_fusion.1 = bf16[48,128,128]{2,1,0:T(8,128)(2,1)S(1)} fusion(bf16[48,192,128]{2,1,0:T(8,128)(2,1)} %gather_fusion, pred[48]{0:T(512)(128)(4,1)S(1)} %get-tuple-element.32, f32[48]{0:T(128)S(1)} %bitcast_select_fusion.2, bf16[48,192,128]{2,1,0:T(8,128)(2,1)} %gather_fusion.1, pred[48]{0:T(512)(128)(4,1)S(1)} %get-tuple-element.46), kind=kOutput, calls=%fused_computation.20 | convolution fusion | flops 305922048 | bytes 6291744 | tf_op jit(solution)/shard_map/while/body/eval_jaxpr/tsa,tsb->sab/dot_general | solution.py:76
  165.2 39.5 %all_to_all.32 = bf16[48,128,128]{2,1,0:T(8,128)(2,1)S(1)} all-to-all(bf16[48,128,128]{2,1,0:T(8,128)(2,1)S(1)} %multiply_convert_fusion.1), channel_id=1, replica_groups=mesh['fsdp'=16,'tensor'=2] {'fsdp'}, dimensions={0} | all-to-all | bytes 3145728 | tf_op jit(solution)/shard_map/all_to_all | solution.py:90
  204.7 0.9 convert_reduce_fusion
  (10 shorter events, 0.0 us)
Async XLA Ops:
  7.2 1.4 copy-start
  7.2 45.5 %all-gather.2.cloned.1.call-start = ((), (), s32[]{:S(2)}) async-start(), calls=%async_computation.3 | async-start | bytes 1671168 | tf_op jit(solution)/shard_map/all_gather | solution.py:48
  106.6 1.8 copy-start.1
  106.6 2.6 %copy-start.2 = (bf16[96,14336]{1,0:T(8,128)(2,1)S(1)}, bf16[96,14336]{1,0:T(8,128)(2,1)}, u32[]{:S(2)}) copy-start(bf16[96,14336]{1,0:T(8,128)(2,1)} %param.8) | copy-start | bytes 8257540
  115.7 5.2 %copy-start.3 = (s32[1,48]{1,0:T(1,128)S(1)}, s32[1,48]{1,0:T(1,128)}, u32[]{:S(2)}) copy-start(s32[1,48]{1,0:T(1,128)} %param.11) | copy-start | bytes 580
  115.7 37.0 %all-to-all-start.1 = ((bf16[96,2,7168]{2,0,1:T(8,128)(2,1)}), bf16[96,2,7168]{2,0,1:T(8,128)(2,1)}, u32[]{:S(2)}, u32[]{:S(2)}) async-start(bf16[96,2,7168]{2,0,1:T(8,128)(2,1)} %bitcast.92), calls=%async_computation.1 | async-start | bytes 5505024 | tf_op jit(solution)/shard_map/all_to_all | solution.py:45
Sparse Core Ops, SparseCore 0:
  10.3 42.3 all-gather.1
where the time goes:
time: 213 us; the launch traced here: 212 us
  blocking collectives  75.9 us (36%)
  waiting for transfers between devices  73.8 us (35%)
  local copies, waits for them, and re-layouts  21.1 us (10%)
  matrix products  15.3 us (7%)
  between operations  14.2 us (7%)
  other arithmetic  6.97 us (3%)
  starting transfers between devices  5.24 us (2%)
    all_gather x1, waiting for transfers between devices, body(): shard_piece = lax.all_gather(w_slots, 'fsdp', axis=1, tiled=True)  41.3 us
    all_to_all x1, blocking collectives, body(): lax.all_to_all(partials, 'fsdp', split_axis=0, concat_axis=0, tiled=True)  39.5 us
    all_to_all x1, blocking collectives, body(): lax.all_to_all(d_hidden, 'tensor', split_axis=0, concat_axis=1, tiled=True)  36.4 us
    all_to_all x1, waiting for transfers between devices, body(): lax.all_to_all(hidden_seq, 'tensor', split_axis=1, concat_axis=0, tiled=T...  31.8 us
    dot_general x1, matrix products, advance(): jnp.einsum('tsa,sr->tra', contrib, onehot, precision=lax.Precision.HIGHEST)  8.27 us
    convert_element_type x1, local copies, waits for them, and re-layouts, body(): d_hidden = running.reshape(token_count, ff_dev).astype(jnp.bfloat16)  5.29 us
    all_to_all x1, starting transfers between devices, body(): lax.all_to_all(hidden_seq, 'tensor', split_axis=1, concat_axis=0, tiled=T...  5.2 us
    convert_element_type x1, other arithmetic, swiglu_grads(): grad_up = (dh_f * (gate_f * gate_sig)).astype(jnp.bfloat16)  4.73 us
  transfers between devices with their start and end apart: 2, of which 2 were waited for; matrix products, arithmetic and copies ran while one was open for 2% of the time, Pallas kernels for 0%

commit v1 on v0

--- a/solution.py
+++ b/solution.py
@@ -1,9 +1,14 @@
+import functools
 import math
 
 import jax
 import jax.numpy as jnp
 from jax import lax
+from jax.experimental import pallas as pl
+from jax.experimental.pallas import tpu as pltpu
 from jax.sharding import PartitionSpec as P
+
+MIB = 1 << 20
 
 
 def swiglu_value(gate_part, up_part):
@@ -22,7 +27,7 @@
     return (grad_gate, grad_up)
 
 
-def body(gate_pre, up_pre, cotangent, w_slots, slot_ids):
+def wide_body(gate_pre, up_pre, cotangent, w_slots, slot_ids):
     n_fsdp = lax.axis_size("fsdp")
     block_size = w_slots.shape[2]
     token_count = cotangent.shape[0]
@@ -98,6 +103,99 @@
     return (d_gate, d_up, w_grad)
 
 
+def partial_kernel(scale, ids_ref, gate_ref, up_ref, cot_ref, out_ref):
+    n_tensor, slots, block, _ = out_ref.shape
+    tokens, ff = gate_ref.shape
+    rows = ff // block // n_tensor
+    cols = cot_ref.shape[1] // block
+    base = pl.multiple_of(lax.axis_index("tensor") * tokens, tokens)
+    for t in range(n_tensor):
+
+        @pl.loop(0, slots, unroll=8)
+        def _(s, t=t):
+            slot = ids_ref[t, s]
+            safe = jnp.maximum(slot, 0)
+            r = pl.multiple_of((safe // cols + t * rows) * block, block)
+            c = pl.multiple_of((safe % cols) * block, block)
+            h = swiglu_value(gate_ref[:, pl.ds(r, block)], up_ref[:, pl.ds(r, block)])
+            dy = cot_ref[pl.ds(base, tokens), pl.ds(c, block)]
+            part = lax.dot_general(h, dy, (((0,), (0,)), ((), ())), preferred_element_type=jnp.float32)
+            out_ref[t, s] = (part * jnp.where(slot >= 0, scale, 0.0)).astype(out_ref.dtype)
+
+
+def grads_kernel(ids_ref, w_ref, cot_ref, gate_ref, up_ref, dgate_ref, dup_ref, dh_ref):
+    n_tensor, slots, block, _ = w_ref.shape
+    steps, tokens, width = dh_ref.shape
+    rows = steps * width // block // n_tensor
+    cols = cot_ref.shape[1] // block
+    per = width // block
+    base = pl.multiple_of(lax.axis_index("tensor") * tokens, tokens)
+    step = pl.program_id(0)
+
+    @pl.when(step == 0)
+    def _():
+        dh_ref[...] = jnp.zeros_like(dh_ref)
+        for t in range(n_tensor):
+
+            @pl.loop(0, slots, unroll=4)
+            def _(s, t=t):
+                slot = ids_ref[t, s]
+                safe = jnp.maximum(slot, 0)
+                r = safe // cols + t * rows
+                c = pl.multiple_of((safe % cols) * block, block)
+                dy = cot_ref[pl.ds(base, tokens), pl.ds(c, block)]
+                add = lax.dot_general(dy, w_ref[t, s], (((1,), (1,)), ((), ())), preferred_element_type=jnp.float32)
+                at = (r // per, slice(None), pl.ds(pl.multiple_of(r % per * block, block), block))
+                dh_ref[at] += jnp.where(slot >= 0, add, 0.0)
+
+    dh = dh_ref[step].astype(jnp.bfloat16)
+    dgate_ref[...], dup_ref[...] = swiglu_grads(dh, gate_ref[...], up_ref[...])
+
+
+def local_partials(ids, gate, up, cot, scale, block):
+    n_tensor, slots = ids.shape
+    whole = pl.BlockSpec(memory_space=pltpu.VMEM)
+    return pl.pallas_call(
+        functools.partial(partial_kernel, scale),
+        out_shape=jax.ShapeDtypeStruct((n_tensor, slots, block, block), jnp.bfloat16),
+        in_specs=[pl.BlockSpec(memory_space=pltpu.SMEM), whole, whole, whole],
+        out_specs=whole,
+        compiler_params=pltpu.CompilerParams(vmem_limit_bytes=40 * MIB),
+    )(ids, gate, up, cot)
+
+
+def local_grads(ids, w_all, cot, gate, up):
+    tokens, ff = gate.shape
+    width = 1024
+    steps = ff // width
+    whole = pl.BlockSpec(memory_space=pltpu.VMEM)
+    tile = pl.BlockSpec((tokens, width), lambda i: (0, i))
+    return pl.pallas_call(
+        grads_kernel,
+        grid=(steps,),
+        out_shape=[jax.ShapeDtypeStruct(gate.shape, jnp.bfloat16)] * 2,
+        in_specs=[pl.BlockSpec(memory_space=pltpu.SMEM), whole, whole, tile, tile],
+        out_specs=[tile, tile],
+        scratch_shapes=[pltpu.VMEM((steps, tokens, width), jnp.float32)],
+        compiler_params=pltpu.CompilerParams(vmem_limit_bytes=40 * MIB),
+    )(ids, w_all, cot, gate, up)
+
+
+def body(gate_pre, up_pre, cotangent, w_slots, slot_ids):
+    n_fsdp = lax.axis_size("fsdp")
+    cap, block = w_slots.shape[1:3]
+    scale = 1.0 / math.sqrt(cotangent.shape[0] * n_fsdp)
+    ids = lax.all_gather(slot_ids, "tensor", axis=0, tiled=True)
+    w_all = lax.all_gather(lax.all_gather(w_slots, "fsdp", axis=1, tiled=True), "tensor", axis=0, tiled=True)
+    partials = local_partials(ids, gate_pre, up_pre, cotangent, scale, block)
+    shares = partials.reshape(2, n_fsdp, cap, block, block).swapaxes(0, 1)
+    shares = shares.reshape(2 * n_fsdp, cap, block, block)
+    arrived = lax.all_to_all(shares, ("fsdp", "tensor"), split_axis=0, concat_axis=0, tiled=True)
+    w_grad = arrived.astype(jnp.float32).sum(axis=0)[None]
+    d_gate, d_up = local_grads(ids, w_all, cotangent, gate_pre, up_pre)
+    return (d_gate, d_up, w_grad)
+
+
 def solution(mesh):
     placed = (
         P(("fsdp", "tensor"), None),
@@ -106,8 +204,9 @@
         P("tensor", "fsdp", None, None),
         P("tensor", None),
     )
+    small = mesh.shape["tensor"] == 2 and mesh.shape["fsdp"] == 16
     return jax.shard_map(
-        body,
+        body if small else wide_body,
         mesh=mesh,
         in_specs=placed,
         out_specs=(

time: 213 us -> 161 us (0.76)
  blocking collectives: 75.9 us -> 5.34 us
  waiting for transfers between devices: 73.8 us -> 102 us
  Pallas kernels: 0 us -> 17.5 us
  matrix products: 15.3 us -> 0 us
  local copies, waits for them, and re-layouts: 21.1 us -> 12.2 us
  other arithmetic: 6.97 us -> 3.16 us
    all_to_all x2 -> x0, blocking collectives: 75.9 us -> none  [the longest x1 39.5 us: body(): lax.all_to_all(partials, 'fsdp', split_axis=0, concat_axis=0, tiled=True)]
    all_gather x1 -> x2, waiting for transfers between devices: 41.3 us -> 76.5 us  [the longest x1 54.9 us: body(): lax.all_gather(w_slots, 'fsdp', axis=1, tiled=True)]
    pallas_call x0 -> x2, Pallas kernels: none -> 17.5 us  [the longest x1 13 us: local_grads(): pl.pallas_call(grads_kernel, grid=(steps,), out_shape=[jax.ShapeDtypeStru...]
    dot_general x3 -> x0, matrix products: 15.3 us -> none  [the longest x1 8.27 us: advance(): jnp.einsum('tsa,sr->tra', contrib, onehot, precision=lax.Precision.HIGHEST)]
    all_to_all x1, waiting for transfers between devices: 31.8 us -> 25 us  [body(): lax.all_to_all(shares, ('fsdp', 'tensor'), split_axis=0, concat_axis=0, t...]
    gather x2 -> x0, local copies, waits for them, and re-layouts: 6.46 us -> none  [the longest x1 4.15 us: partial_group(): h_picked = jnp.take(hidden_blocks, rows_now, axis=1)]
    convert_element_type x2 -> x0, local copies, waits for them, and re-layouts: 5.83 us -> none  [the longest x1 5.29 us: body(): d_hidden = running.reshape(token_count, ff_dev).astype(jnp.bfloat16)]
    unnamed x9 -> x14, local copies, waits for them, and re-layouts: 4.35 us -> 10 us
  transfers between devices with their start and end apart: 2 -> 3, of which waited for: 2 -> 3; matrix products, arithmetic and copies ran while one was open for 2% -> 2% of each run, Pallas kernels for 0% -> 0%
where the time goes in v1:
time: 161 us
  waiting for transfers between devices  102 us (63%)
  Pallas kernels  17.5 us (11%)
  between operations  14.1 us (9%)
  local copies, waits for them, and re-layouts  12.2 us (8%)
  starting transfers between devices  6.5 us (4%)
  blocking collectives  5.34 us (3%)
  other arithmetic  3.16 us (2%)
    all_gather x1, waiting for transfers between devices, body(): lax.all_gather(w_slots, 'fsdp', axis=1, tiled=True)  54.9 us
    all_to_all x1, waiting for transfers between devices, body(): lax.all_to_all(shares, ('fsdp', 'tensor'), split_axis=0, concat_axis=0, t...  25 us
    all_gather x1, waiting for transfers between devices, body(): lax.all_gather(lax.all_gather(w_slots, 'fsdp', axis=1, tiled=True), 'tens...  21.6 us
    pallas_call x1, Pallas kernels, local_grads(): pl.pallas_call(grads_kernel, grid=(steps,), out_shape=[jax.ShapeDtypeStru...  13 us
    unnamed x14, local copies, waits for them, and re-layouts  10 us
    all_to_all x1, starting transfers between devices, body(): lax.all_to_all(shares, ('fsdp', 'tensor'), split_axis=0, concat_axis=0, t...  6.42 us
    all_gather x1, blocking collectives, body(): ids = lax.all_gather(slot_ids, 'tensor', axis=0, tiled=True)  5.34 us
    pallas_call x1, Pallas kernels, local_partials(): pl.pallas_call(functools.partial(partial_kernel, scale), out_shape=jax.Sh...  4.48 us
  transfers between devices with their start and end apart: 3, of which 3 were waited for; matrix products, arithmetic and copies ran while one was open for 2% of the time, Pallas kernels for 0%

profile of v1, /device:TPU:0, one launch (start us, length us, event | category | flops | bytes accessed | tf_op | source)
XLA Modules:
  0.0 161.0 jit_solution(16035746033846602663)
XLA Ops:
  7.2 5.3 %all-gather = s32[2,1,48]{2,1,0:T(1,128)S(1)} all-gather(s32[1,1,48]{2,1,0:T(1,128)} %bitcast.16), channel_id=1, replica_groups=mesh['fsdp'=16,'tensor'=2] {'tensor'}, dimensions={0}, use_global_device_ids=true | all-gather | bytes 576 | tf_op jit(solution)/shard_map/all_gather | solution.py:188
  12.5 0.0 copy-start
  12.5 1.8 %copy-done = bf16[96,14336]{1,0:T(8,128)(2,1)S(1)} copy-done((bf16[96,14336]{1,0:T(8,128)(2,1)S(1)}, bf16[96,14336]{1,0:T(8,128)(2,1)}, u32[]{:S(2)}) %copy-start) | copy-done | bytes 2752536
  14.3 0.0 copy-start.2
  14.3 1.8 %copy-done.2 = bf16[96,14336]{1,0:T(8,128)(2,1)S(1)} copy-done((bf16[96,14336]{1,0:T(8,128)(2,1)S(1)}, bf16[96,14336]{1,0:T(8,128)(2,1)}, u32[]{:S(2)}) %copy-start.2) | copy-done | bytes 2752536
  16.1 0.0 copy-start.4
  16.1 1.4 copy-done.4
  17.5 4.5 %shard_map.77 = bf16[2,48,128,128]{3,2,1,0:T(8,128)(2,1)S(1)} custom-call(s32[2,48]{1,0:T(2,128)S(1)} %bitcast.10, bf16[96,14336]{1,0:T(8,128)(2,1)S(1)} %copy-done, bf16[96,14336]{1,0:T(8,128)(2,1)S(1)} %copy-done.2, bf16[192,4096]{1,0:T(8,128)(2,1)S(1)} %copy-done.4), custom_call_target="tpu_custom_call" | custom-call | tf_op jit(solution)/shard_map/pallas_call | solution.py:158
  22.0 2.1 %copy.11 = bf16[2,16,3,128,128]{4,3,2,0,1:T(8,128)(2,1)} copy(bf16[2,16,3,128,128]{4,3,2,1,0:T(8,128)(2,1)S(1)} %bitcast.9) | data formatting | bytes 6291456 | tf_op jit(solution)/shard_map/reshape | solution.py:191
  24.1 6.4 %all-to-all-start = ((bf16[32,3,128,128]{3,2,1,0:T(8,128)(2,1)}), bf16[32,3,128,128]{3,2,1,0:T(8,128)(2,1)}, u32[]{:S(2)}, u32[]{:S(2)}) async-start(bf16[32,3,128,128]{3,2,1,0:T(8,128)(2,1)} %bitcast.12), calls=%async_computation | async-start | bytes 6291456 | tf_op jit(solution)/shard_map/all_to_all | solution.py:193
  30.5 0.0 copy-start.1
  30.5 0.0 all-gather.4.cloned.1.call-start
  30.6 0.7 all-gather.4.cloned.1.call-update
  31.3 0.0 all-gather.6.cloned.1.call-start
  31.3 54.9 %all-gather.4.cloned.1.call-done = bf16[1,48,128,128]{3,2,0,1:T(8,128)(2,1)} async-done(((bf16[1,3,128,128]{3,2,0,1:T(8,128)(2,1)}), bf16[1,48,128,128]{3,2,0,1:T(8,128)(2,1)}) %all-gather.4.cloned.1.call-update) | async-done | bytes 1572880 | tf_op jit(solution)/shard_map/all_gather | solution.py:189
  86.2 0.0 all-gather.6.cloned.1.call-update
  86.2 25.0 %all-to-all-done = bf16[32,3,128,128]{3,2,1,0:T(8,128)(2,1)} async-done(((bf16[32,3,128,128]{3,2,1,0:T(8,128)(2,1)}), bf16[32,3,128,128]{3,2,1,0:T(8,128)(2,1)}, u32[]{:S(2)}, u32[]{:S(2)}) %all-to-all-start) | async-done | bytes 3145760 | tf_op jit(solution)/shard_map/all_to_all | solution.py:193
  111.2 3.2 %convert_reduce_fusion = f32[3,128,128]{2,1,0:T(8,128)} fusion(bf16[32,3,128,128]{3,2,1,0:T(8,128)(2,1)} %all-to-all-done), kind=kLoop, calls=%fused_computation | loop fusion | flops 3096576 | bytes 3342336 | tf_op jit(solution)/shard_map/reduce_sum | solution.py:194
  114.4 21.6 %all-gather.6.cloned.1.call-done.w_ref = bf16[2,48,128,128]{3,2,1,0:T(8,128)(2,1)} async-done(((bf16[1,48,128,128]{3,2,1,0:T(8,128)(2,1)}), bf16[2,48,128,128]{3,2,1,0:T(8,128)(2,1)}) %all-gather.6.cloned.1.call-update) | async-done | bytes 3145744 | tf_op jit(solution)/shard_map/all_gather | solution.py:189
  136.0 0.0 copy-done.1
  136.0 1.8 %copy-done.3 = bf16[96,14336]{1,0:T(8,128)(2,1)S(1)} copy-done((bf16[96,14336]{1,0:T(8,128)(2,1)S(1)}, bf16[96,14336]{1,0:T(8,128)(2,1)}, u32[]{:S(2)}) %copy-start.3) | copy-done | bytes 2752536
  137.8 1.4 copy-done.5
  139.2 1.9 %copy-done.6 = bf16[2,48,128,128]{3,2,1,0:T(8,128)(2,1)S(1)} copy-done((bf16[2,48,128,128]{3,2,1,0:T(8,128)(2,1)S(1)}, bf16[2,48,128,128]{3,2,1,0:T(8,128)(2,1)}, u32[]{:S(2)}) %copy-start.6) | copy-done | bytes 3145752
  141.1 13.0 %shard_map.76 = (bf16[96,14336]{1,0:T(8,128)(2,1)}, bf16[96,14336]{1,0:T(8,128)(2,1)}) custom-call(s32[2,48]{1,0:T(2,128)S(1)} %bitcast.11, bf16[2,48,128,128]{3,2,1,0:T(8,128)(2,1)S(1)} %copy-done.6, bf16[192,4096]{1,0:T(8,128)(2,1)S(1)} %copy-done.5, bf16[96,14336]{1,0:T(8,128)(2,1)S(1)} %copy-done.1, bf16[96,14336]{1,0:T(8,128)(2,1)S(1)} %copy-done.3), custom_call_target="tpu_custom_call" | custom-call | tf_op jit(solution)/shard_map/pallas_call | solution.py:173
  (3 shorter events, 0.0 us)
Async XLA Ops:
  12.5 1.8 %copy-start = (bf16[96,14336]{1,0:T(8,128)(2,1)S(1)}, bf16[96,14336]{1,0:T(8,128)(2,1)}, u32[]{:S(2)}) copy-start(bf16[96,14336]{1,0:T(8,128)(2,1)} %gate_ref.3) | copy-start | bytes 8257540
  14.3 1.8 %copy-start.2 = (bf16[96,14336]{1,0:T(8,128)(2,1)S(1)}, bf16[96,14336]{1,0:T(8,128)(2,1)}, u32[]{:S(2)}) copy-start(bf16[96,14336]{1,0:T(8,128)(2,1)} %up_ref.3) | copy-start | bytes 8257540
  16.1 1.4 copy-start.4
  24.1 87.1 %all-to-all-start = ((bf16[32,3,128,128]{3,2,1,0:T(8,128)(2,1)}), bf16[32,3,128,128]{3,2,1,0:T(8,128)(2,1)}, u32[]{:S(2)}, u32[]{:S(2)}) async-start(bf16[32,3,128,128]{3,2,1,0:T(8,128)(2,1)} %bitcast.12), calls=%async_computation | async-start | bytes 6291456 | tf_op jit(solution)/shard_map/all_to_all | solution.py:193
  30.5 105.5 %copy-start.1 = (bf16[96,14336]{1,0:T(8,128)(2,1)S(1)}, bf16[96,14336]{1,0:T(8,128)(2,1)}, u32[]{:S(2)}) copy-start(bf16[96,14336]{1,0:T(8,128)(2,1)} %gate_ref.3) | copy-start | bytes 8257540
  30.5 55.7 %all-gather.4.cloned.1.call-start = ((), (), s32[]{:S(2)}) async-start(), calls=%async_computation.1 | async-start | bytes 1671168 | tf_op jit(solution)/shard_map/all_gather | solution.py:189
  31.3 104.8 %all-gather.6.cloned.1.call-start = ((), (), s32[]{:S(2)}) async-start(), calls=%async_computation.2 | async-start | bytes 4718592 | tf_op jit(solution)/shard_map/all_gather | solution.py:189
  136.0 1.8 %copy-start.3 = (bf16[96,14336]{1,0:T(8,128)(2,1)S(1)}, bf16[96,14336]{1,0:T(8,128)(2,1)}, u32[]{:S(2)}) copy-start(bf16[96,14336]{1,0:T(8,128)(2,1)} %up_ref.3) | copy-start | bytes 8257540
  137.8 1.4 copy-start.5
  139.2 1.9 %copy-start.6 = (bf16[2,48,128,128]{3,2,1,0:T(8,128)(2,1)S(1)}, bf16[2,48,128,128]{3,2,1,0:T(8,128)(2,1)}, u32[]{:S(2)}) copy-start(bf16[2,48,128,128]{3,2,1,0:T(8,128)(2,1)} %all-gather.6.cloned.1.call-done.w_ref) | copy-start | bytes 9437188
Sparse Core Ops, SparseCore 0:
  33.7 52.4 all-gather.3
  87.7 48.2 all-gather.5

commit v2 on v0

--- a/solution.py
+++ b/solution.py
@@ -1,9 +1,14 @@
+import functools
 import math
 
 import jax
 import jax.numpy as jnp
 from jax import lax
+from jax.experimental import pallas as pl
+from jax.experimental.pallas import tpu as pltpu
 from jax.sharding import PartitionSpec as P
+
+MIB = 1 << 20
 
 
 def swiglu_value(gate_part, up_part):
@@ -22,7 +27,7 @@
     return (grad_gate, grad_up)
 
 
-def body(gate_pre, up_pre, cotangent, w_slots, slot_ids):
+def wide_body(gate_pre, up_pre, cotangent, w_slots, slot_ids):
     n_fsdp = lax.axis_size("fsdp")
     block_size = w_slots.shape[2]
     token_count = cotangent.shape[0]
@@ -98,6 +103,294 @@
     return (d_gate, d_up, w_grad)
 
 
+def exchange_kernel(
+    scale, ids_ref, ids_vec, gate_hbm, up_hbm, cot_hbm, w_hbm,
+    ids_other, con_ref, wgrad_ref,
+    ids_in, gate, up, cot, w_all, part, rc, rx0, ry1, ry0, rx1, rz, local, send, recv,
+):
+    tokens = gate.shape[1]
+    cap, block, _ = w_hbm.shape[1:]
+    n_z = w_all.shape[3]
+    half = block // 2
+    cols = cot.shape[0]
+    rows = gate.shape[0] // 2
+    f = lax.axis_index("fsdp")
+    y = lax.axis_index("tensor")
+    z, x, k = f // 4, f // 2 % 2, f % 2
+    to_core = {"fsdp": f + 1 - 2 * k, "tensor": y}
+    to_x = {"fsdp": f + 2 - 4 * x, "tensor": y}
+    to_y = {"fsdp": f, "tensor": 1 - y}
+    to_z = [{"fsdp": (z + d) % n_z * 4 + x * 2 + k, "tensor": y} for d in range(1, n_z)]
+    part_rows = [pl.ds(0, half), pl.ds(half, half)]
+
+    def copy(i, src, dst, to):
+        return pltpu.make_async_remote_copy(
+            src_ref=src, dst_ref=dst, send_sem=send.at[i], recv_sem=recv.at[i],
+            device_id=to, device_id_type=pl.DeviceIdType.MESH,
+        )
+
+    def same(i, ref, to):
+        return copy(i, ref, ref, to)
+
+    own_w = pltpu.make_async_copy(w_hbm.at[0], w_all.at[k, y, x, z], local.at[3])
+    own_w.start()
+    own_tokens = pl.ds(pl.multiple_of(y * tokens, tokens), tokens)
+
+    @pl.loop(0, cols)
+    def _(i):
+        at = pl.ds(pl.multiple_of(i * block, block), block)
+        pltpu.make_async_copy(cot_hbm.at[own_tokens, at], cot.at[i], local.at[2]).start()
+
+    @pl.loop(0, 2 * rows)
+    def _(i):
+        at = pl.ds(pl.multiple_of(i * block, block), block)
+        pltpu.make_async_copy(gate_hbm.at[:, at], gate.at[i], local.at[0]).start()
+        pltpu.make_async_copy(up_hbm.at[:, at], up.at[i], local.at[1]).start()
+
+    barrier = pltpu.get_barrier_semaphore()
+    peers = [to_core, to_x, to_y] + to_z
+    for to in peers:
+        pl.semaphore_signal(barrier, inc=1, device_id=to, device_id_type=pl.DeviceIdType.MESH)
+    pl.semaphore_wait(barrier, len(peers))
+
+    ids_copy = copy(0, ids_vec, ids_in, to_y)
+    ids_copy.start()
+    ag_z = [copy(1 + d, w_hbm.at[0], w_all.at[k, y, x, z], to_z[d]) for d in range(n_z - 1)]
+    for c in ag_z:
+        c.start()
+    for n, ref in enumerate((gate, up, cot)):
+        pltpu.make_async_copy(ref, ref, local.at[n]).wait()
+    own_w.wait()
+
+    def partials(core, t, ids):
+        @pl.loop(0, 2 * n_z * cap, unroll=8)
+        def _(i):
+            q, zz, xx = i % cap, i // cap % n_z, i // (cap * n_z)
+            slot = ids[0, (zz * 4 + xx * 2 + core) * cap + q]
+            safe = lax.max(slot, 0)
+            r = lax.div(safe, cols) + t * rows
+            c = lax.rem(safe, cols)
+            usable = lax.min(slot + 1, 1).astype(jnp.float32)
+            h = swiglu_value(gate[r], up[r])
+            dy = cot[c]
+            got = lax.dot_general(h, dy, (((0,), (0,)), ((), ())), preferred_element_type=jnp.float32)
+            part[core, t, xx, zz, q] = (got * (usable * scale)).astype(part.dtype)
+
+    def contribs(core, t, xx, ids):
+        @pl.loop(0, n_z * cap, unroll=6)
+        def _(i):
+            q, zz = i % cap, i // cap
+            slot = ids[0, (zz * 4 + xx * 2 + core) * cap + q]
+            c = lax.rem(lax.max(slot, 0), cols)
+            usable = lax.min(slot + 1, 1).astype(jnp.float32)
+            got = lax.dot_general(
+                cot[c], w_all[core, t, xx, zz, q], (((1,), (1,)), ((), ())),
+                preferred_element_type=jnp.float32,
+            )
+            con_ref[core, t, xx, zz, q] = (got * usable).astype(con_ref.dtype)
+
+    def add(dst, src):
+        total = dst[...].astype(jnp.float32) + src[...].astype(jnp.float32)
+        dst[...] = total.astype(dst.dtype)
+
+    partials(1 - k, y, ids_ref)
+    core_p = [copy(13, part.at[1 - k, y], rc.at[y], to_core)]
+    core_p[0].start()
+    ids_copy.wait_recv()
+    ids_local = pltpu.make_async_copy(ids_in, ids_other, local.at[4])
+    ids_local.start()
+    ids_local.wait()
+    partials(1 - k, 1 - y, ids_other)
+    core_p.append(copy(14, part.at[1 - k, 1 - y], rc.at[1 - y], to_core))
+    core_p[1].start()
+    partials(k, y, ids_ref)
+    partials(k, 1 - y, ids_other)
+
+    for c in ag_z:
+        c.wait_recv()
+    core_w = [same(4, w_all.at[k, y, x], to_core)]
+    ag_x0 = same(5, w_all.at[k, y, x, :, :, part_rows[0]], to_x)
+    ag_y1 = same(6, w_all.at[k, y, x, :, :, part_rows[1]], to_y)
+    ag_x0.start()
+    ag_y1.start()
+    core_w[0].start()
+
+    for n, t in enumerate((y, 1 - y)):
+        core_p[n].wait_recv()
+
+        @pl.loop(0, 2 * n_z)
+        def _(i, t=t):
+            at = (t, i // n_z, i % n_z)
+            add(part.at[(k,) + at], rc.at[at])
+
+    rs_x0 = copy(15, part.at[k, :, 1 - x, :, :, part_rows[0]], rx0, to_x)
+    rs_y1 = copy(16, part.at[k, 1 - y, :, :, :, part_rows[1]], ry1, to_y)
+    rs_x0.start()
+    rs_y1.start()
+
+    ag_x0.wait_recv()
+    ag_y0 = same(9, w_all.at[k, y, :, :, :, part_rows[0]], to_y)
+    ag_y0.start()
+    core_w.append(same(7, w_all.at[k, y, 1 - x, :, :, part_rows[0]], to_core))
+    core_w[1].start()
+    ag_y1.wait_recv()
+    ag_x1 = same(10, w_all.at[k, :, x, :, :, part_rows[1]], to_x)
+    ag_x1.start()
+    core_w.append(same(8, w_all.at[k, 1 - y, x, :, :, part_rows[1]], to_core))
+    core_w[2].start()
+
+    contribs(k, y, x, ids_ref)
+    core_w[0].wait_recv()
+    contribs(1 - k, y, x, ids_ref)
+
+    rs_x0.wait_recv()
+
+    @pl.loop(0, 2 * n_z)
+    def _(i):
+        add(part.at[k, i // n_z, x, i % n_z, :, part_rows[0]], rx0.at[i // n_z, i % n_z])
+
+    rs_y0 = copy(17, part.at[k, 1 - y, x, :, :, part_rows[0]], ry0, to_y)
+    rs_y0.start()
+    rs_y1.wait_recv()
+
+    @pl.loop(0, 2 * n_z)
+    def _(i):
+        add(part.at[k, y, i // n_z, i % n_z, :, part_rows[1]], ry1.at[i // n_z, i % n_z])
+
+    rs_x1 = copy(18, part.at[k, y, 1 - x, :, :, part_rows[1]], rx1, to_x)
+    rs_x1.start()
+
+    ag_y0.wait_recv()
+    core_w.append(same(11, w_all.at[k, 1 - y, :, :, :, part_rows[0]], to_core))
+    core_w[3].start()
+    ag_x1.wait_recv()
+    core_w.append(same(12, w_all.at[k, :, 1 - x, :, :, part_rows[1]], to_core))
+    core_w[4].start()
+
+    rs_z = []
+    for p, came, into in ((0, rs_y0, ry0), (1, rs_x1, rx1)):
+        came.wait_recv()
+
+        @pl.loop(0, n_z)
+        def _(i, p=p, into=into):
+            add(part.at[k, y, x, i, :, part_rows[p]], into.at[i])
+
+        for d in range(n_z - 1):
+            c = copy(19 + p * (n_z - 1) + d, part.at[k, y, x, (z + d + 1) % n_z, :, part_rows[p]], rz.at[d, p], to_z[d])
+            c.start()
+            rs_z.append(c)
+
+    contribs(k, y, 1 - x, ids_ref)
+    contribs(k, 1 - y, x, ids_other)
+    contribs(k, 1 - y, 1 - x, ids_other)
+    for c in core_w[1:]:
+        c.wait_recv()
+    contribs(1 - k, y, 1 - x, ids_ref)
+    contribs(1 - k, 1 - y, x, ids_other)
+    contribs(1 - k, 1 - y, 1 - x, ids_other)
+
+    for c in rs_z:
+        c.wait_recv()
+    for p in range(2):
+        total = part[k, y, x, z, :, part_rows[p]].astype(jnp.float32)
+        for d in range(n_z - 1):
+            total = total + rz[d, p].astype(jnp.float32)
+        wgrad_ref[0, :, part_rows[p]] = total
+    for c in [ids_copy, ag_x0, ag_y1, ag_y0, ag_x1, rs_x0, rs_y1, rs_y0, rs_x1] + ag_z + core_p + core_w + rs_z:
+        c.wait_send()
+
+
+def exchange(gate, up, cot, w, ids, scale):
+    tokens, ff = gate.shape
+    cap, block = w.shape[1:3]
+    bf16 = jnp.bfloat16
+    any_spec = pl.BlockSpec(memory_space=pl.ANY)
+    smem = pl.BlockSpec(memory_space=pltpu.SMEM)
+    whole = pl.BlockSpec(memory_space=pltpu.VMEM)
+    n_z = lax.axis_size("fsdp") // 4
+    half = block // 2
+    return pl.pallas_call(
+        functools.partial(exchange_kernel, scale),
+        out_shape=[
+            jax.ShapeDtypeStruct(ids.shape, ids.dtype),
+            jax.ShapeDtypeStruct((2, 2, 2, n_z, cap, tokens, block), bf16),
+            jax.ShapeDtypeStruct(w.shape, jnp.float32),
+        ],
+        in_specs=[smem, whole, any_spec, any_spec, any_spec, any_spec],
+        out_specs=[smem, whole, whole],
+        scratch_shapes=[
+            pltpu.VMEM(ids.shape, ids.dtype),
+            pltpu.VMEM((ff // block, tokens, block), bf16),
+            pltpu.VMEM((ff // block, tokens, block), bf16),
+            pltpu.VMEM((cot.shape[1] // block, tokens, block), bf16),
+            pltpu.VMEM((2, 2, 2, n_z, cap, block, block), bf16),
+            pltpu.VMEM((2, 2, 2, n_z, cap, block, block), bf16),
+            pltpu.VMEM((2, 2, n_z, cap, block, block), bf16),
+            pltpu.VMEM((2, n_z, cap, half, block), bf16),
+            pltpu.VMEM((2, n_z, cap, half, block), bf16),
+            pltpu.VMEM((n_z, cap, half, block), bf16),
+            pltpu.VMEM((n_z, cap, half, block), bf16),
+            pltpu.VMEM((n_z - 1, 2, cap, half, block), bf16),
+            pltpu.SemaphoreType.DMA((5,)),
+            pltpu.SemaphoreType.DMA((19 + 2 * (n_z - 1),)),
+            pltpu.SemaphoreType.DMA((19 + 2 * (n_z - 1),)),
+        ],
+        compiler_params=pltpu.CompilerParams(
+            collective_id=0, has_side_effects=True, vmem_limit_bytes=48 * MIB
+        ),
+    )(ids, ids, gate, up, cot, w)
+
+
+def grads_kernel(cols, ids_ref, other_ref, con_ref, gate_ref, up_ref, dgate_ref, dup_ref, dh_ref):
+    n_z, cap, tokens, block = con_ref.shape[3:]
+    steps, _, width = dh_ref.shape
+    per = width // block
+    rows = steps * per // 2
+    y = lax.axis_index("tensor")
+    step = pl.program_id(0)
+
+    @pl.when(step == 0)
+    def _():
+        dh_ref[...] = jnp.zeros_like(dh_ref)
+        for t, ids in ((y, ids_ref), (1 - y, other_ref)):
+
+            @pl.loop(0, 4 * n_z * cap, unroll=4)
+            def _(s, t=t, ids=ids):
+                slot = ids[0, s]
+                f = s // cap
+                r = jnp.maximum(slot, 0) // cols + t * rows
+                at = (r // per, slice(None), pl.ds(pl.multiple_of(r % per * block, block), block))
+                dh_ref[at] += con_ref[f % 2, t, f // 2 % 2, f // 4, s % cap].astype(jnp.float32)
+
+    dh = dh_ref[step].astype(jnp.bfloat16)
+    dgate_ref[...], dup_ref[...] = swiglu_grads(dh, gate_ref[...], up_ref[...])
+
+
+def local_grads(ids, other, contrib, cols, gate, up):
+    tokens, ff = gate.shape
+    width = 1024
+    steps = ff // width
+    smem = pl.BlockSpec(memory_space=pltpu.SMEM)
+    tile = pl.BlockSpec((tokens, width), lambda i: (0, i))
+    return pl.pallas_call(
+        functools.partial(grads_kernel, cols),
+        grid=(steps,),
+        out_shape=[jax.ShapeDtypeStruct(gate.shape, jnp.bfloat16)] * 2,
+        in_specs=[smem, smem, pl.BlockSpec(memory_space=pltpu.VMEM), tile, tile],
+        out_specs=[tile, tile],
+        scratch_shapes=[pltpu.VMEM((steps, tokens, width), jnp.float32)],
+        compiler_params=pltpu.CompilerParams(vmem_limit_bytes=40 * MIB),
+    )(ids, other, contrib, gate, up)
+
+
+def body(gate_pre, up_pre, cotangent, w_slots, slot_ids):
+    scale = 1.0 / math.sqrt(cotangent.shape[0] * lax.axis_size("fsdp"))
+    other, contrib, w_grad = exchange(gate_pre, up_pre, cotangent, w_slots, slot_ids, scale)
+    cols = cotangent.shape[1] // w_slots.shape[2]
+    d_gate, d_up = local_grads(slot_ids, other, contrib, cols, gate_pre, up_pre)
+    return (d_gate, d_up, w_grad)
+
+
 def solution(mesh):
     placed = (
         P(("fsdp", "tensor"), None),
@@ -106,8 +399,9 @@
         P("tensor", "fsdp", None, None),
         P("tensor", None),
     )
+    small = mesh.shape["tensor"] == 2 and mesh.shape["fsdp"] == 16
     return jax.shard_map(
-        body,
+        body if small else wide_body,
         mesh=mesh,
         in_specs=placed,
         out_specs=(

time: 213 us -> 67.6 us (0.32)
  blocking collectives: 75.9 us -> 0 us
  waiting for transfers between devices: 73.8 us -> 0 us
  Pallas kernels: 0 us -> 62.4 us
  local copies, waits for them, and re-layouts: 21.1 us -> 4.31 us
  matrix products: 15.3 us -> 0 us
  between operations: 14.2 us -> 0.68 us
  other arithmetic: 6.97 us -> 0 us
  starting transfers between devices: 5.24 us -> 0 us
    all_to_all x2 -> x0, blocking collectives: 75.9 us -> none  [the longest x1 39.5 us: body(): lax.all_to_all(partials, 'fsdp', split_axis=0, concat_axis=0, tiled=True)]
    pallas_call x0 -> x2, Pallas kernels: none -> 62.4 us  [the longest x1 51.5 us: exchange(): pl.pallas_call(functools.partial(exchange_kernel, scale), out_shape=[jax....]
    all_gather x1 -> x0, waiting for transfers between devices: 41.3 us -> none  [body(): shard_piece = lax.all_gather(w_slots, 'fsdp', axis=1, tiled=True)]
    all_to_all x1 -> x0, waiting for transfers between devices: 31.8 us -> none  [body(): lax.all_to_all(hidden_seq, 'tensor', split_axis=1, concat_axis=0, tiled=T...]
    dot_general x3 -> x0, matrix products: 15.3 us -> none  [the longest x1 8.27 us: advance(): jnp.einsum('tsa,sr->tra', contrib, onehot, precision=lax.Precision.HIGHEST)]
    gather x2 -> x0, local copies, waits for them, and re-layouts: 6.46 us -> none  [the longest x1 4.15 us: partial_group(): h_picked = jnp.take(hidden_blocks, rows_now, axis=1)]
    convert_element_type x2 -> x0, local copies, waits for them, and re-layouts: 5.83 us -> none  [the longest x1 5.29 us: body(): d_hidden = running.reshape(token_count, ff_dev).astype(jnp.bfloat16)]
    all_to_all x1 -> x0, starting transfers between devices: 5.2 us -> none  [body(): lax.all_to_all(hidden_seq, 'tensor', split_axis=1, concat_axis=0, tiled=T...]
  transfers between devices with their start and end apart: 2 -> 0, of which waited for: 2 -> 0; matrix products, arithmetic and copies ran while one was open for 2% -> 0% of each run, Pallas kernels for 0% -> 0%
where the time goes in v2:
time: 67.6 us; the launch traced here: 67.4 us
  Pallas kernels  62.4 us (92%)
  local copies, waits for them, and re-layouts  4.31 us (6%)
  between operations  0.68 us (1%)
    pallas_call x1, Pallas kernels, exchange(): pl.pallas_call(functools.partial(exchange_kernel, scale), out_shape=[jax....  51.5 us
    pallas_call x1, Pallas kernels, local_grads(): pl.pallas_call(functools.partial(grads_kernel, cols), grid=(steps,), out_...  10.9 us
    unnamed x11, local copies, waits for them, and re-layouts  4.31 us

profile of v2, /device:TPU:0, one launch (start us, length us, event | category | flops | bytes accessed | tf_op | source)
XLA Modules:
  0.0 67.4 jit_solution(1184974189343880171)
XLA Ops:
  0.6 0.0 copy-start.1
  0.6 0.0 copy-start
  0.7 0.0 copy-start.2
  0.7 1.5 %copy-done.2 = bf16[192,4096]{1,0:T(8,128)(2,1)S(1)} copy-done((bf16[192,4096]{1,0:T(8,128)(2,1)S(1)}, bf16[192,4096]{1,0:T(8,128)(2,1)}, u32[]{:S(2)}) %copy-start.2) | copy-done | bytes 1572888
  2.2 0.0 copy-start.3
  2.2 1.4 %copy-done.3 = bf16[1,3,128,128]{3,2,1,0:T(8,128)(2,1)S(1)} copy-done((bf16[1,3,128,128]{3,2,1,0:T(8,128)(2,1)S(1)}, bf16[1,3,128,128]{3,2,1,0:T(8,128)(2,1)}, u32[]{:S(2)}) %copy-start.3) | copy-done | bytes 98328
  3.6 0.0 copy-start.4
  3.6 0.7 copy-done.4
  4.3 51.5 %shard_map.76 = (s32[1,48]{1,0:T(1,128)S(1)}, bf16[2,2,2,4,3,96,128]{6,5,4,3,2,1,0:T(8,128)(2,1)S(1)}, f32[1,3,128,128]{3,2,1,0:T(8,128)S(1)}) custom-call(s32[1,48]{1,0:T(1,128)S(1)} %copy-done.4, s32[1,48]{1,0:T(1,128)S(1)} %copy-done.4, bf16[96,14336]{1,0:T(8,128)(2,1)} %gate_ref.1, bf16[96,14336]{1,0:T(8,128)(2,1)} %up_ref.1, ...), custom_call_target="tpu_custom_call" | custom-call | tf_op jit(solution)/shard_map/pallas_call | solution.py:312
  55.8 0.0 copy-done.1
  55.8 0.0 copy-done
  55.8 10.9 %shard_map.77 = (bf16[96,14336]{1,0:T(8,128)(2,1)}, bf16[96,14336]{1,0:T(8,128)(2,1)}) custom-call(s32[1,48]{1,0:T(1,128)S(1)} %copy-done.4, s32[1,48]{1,0:T(1,128)S(1)} %get-tuple-element.8.other_ref, bf16[2,2,2,4,3,96,128]{6,5,4,3,2,1,0:T(8,128)(2,1)S(1)} %get-tuple-element.9.con_ref, bf16[96,14336]{1,0:T(8,128)(2,1)S(1)} %copy-done, ...), custom_call_target="tpu_custom_call" | custom-call | tf_op jit(solution)/shard_map/pallas_call | solution.py:375
  66.7 0.7 %copy.9 = f32[1,3,128,128]{3,2,1,0:T(8,128)} copy(f32[1,3,128,128]{3,2,1,0:T(8,128)S(1)} %get-tuple-element.18) | data formatting | bytes 393216
Async XLA Ops:
  0.6 55.2 %copy-start.1 = (bf16[96,14336]{1,0:T(8,128)(2,1)S(1)}, bf16[96,14336]{1,0:T(8,128)(2,1)}, u32[]{:S(2)}) copy-start(bf16[96,14336]{1,0:T(8,128)(2,1)} %up_ref.1) | copy-start | bytes 8257540
  0.6 55.2 %copy-start = (bf16[96,14336]{1,0:T(8,128)(2,1)S(1)}, bf16[96,14336]{1,0:T(8,128)(2,1)}, u32[]{:S(2)}) copy-start(bf16[96,14336]{1,0:T(8,128)(2,1)} %gate_ref.1) | copy-start | bytes 8257540
  0.7 1.6 %copy-start.2 = (bf16[192,4096]{1,0:T(8,128)(2,1)S(1)}, bf16[192,4096]{1,0:T(8,128)(2,1)}, u32[]{:S(2)}) copy-start(bf16[192,4096]{1,0:T(8,128)(2,1)} %cot_hbm.1) | copy-start | bytes 4718596
  2.2 1.4 %copy-start.3 = (bf16[1,3,128,128]{3,2,1,0:T(8,128)(2,1)S(1)}, bf16[1,3,128,128]{3,2,1,0:T(8,128)(2,1)}, u32[]{:S(2)}) copy-start(bf16[1,3,128,128]{3,2,1,0:T(8,128)(2,1)} %w_hbm.1) | copy-start | bytes 294916
  3.6 0.7 copy-start.4

commit v3 on v2

--- a/solution.py
+++ b/solution.py
@@ -103,6 +103,15 @@
     return (d_gate, d_up, w_grad)
 
 
+def sigmoid(value):
+    return 0.5 + 0.5 * jnp.tanh(0.5 * value)
+
+
+def hidden_value(gate_part, up_part):
+    gate_f = gate_part.astype(jnp.float32)
+    return (gate_f * sigmoid(gate_f) * up_part.astype(jnp.float32)).astype(jnp.bfloat16)
+
+
 def exchange_kernel(
     scale, ids_ref, ids_vec, gate_hbm, up_hbm, cot_hbm, w_hbm,
     ids_other, con_ref, wgrad_ref,
@@ -132,46 +141,63 @@
     def same(i, ref, to):
         return copy(i, ref, ref, to)
 
-    own_w = pltpu.make_async_copy(w_hbm.at[0], w_all.at[k, y, x, z], local.at[3])
-    own_w.start()
+    barrier = pltpu.get_barrier_semaphore()
+    peers = [to_core, to_x, to_y] + to_z
+    for to in peers:
+        pl.semaphore_signal(barrier, inc=1, device_id=to, device_id_type=pl.DeviceIdType.MESH)
     own_tokens = pl.ds(pl.multiple_of(y * tokens, tokens), tokens)
 
-    @pl.loop(0, cols)
+    @pl.loop(0, cols, unroll=4)
     def _(i):
         at = pl.ds(pl.multiple_of(i * block, block), block)
         pltpu.make_async_copy(cot_hbm.at[own_tokens, at], cot.at[i], local.at[2]).start()
 
-    @pl.loop(0, 2 * rows)
+    own_w = pltpu.make_async_copy(w_hbm.at[0], w_all.at[k, y, x, z], local.at[3])
+    own_w.start()
+    pl.semaphore_wait(barrier, len(peers))
+
+    ids_copy = copy(0, ids_vec, ids_in, to_y)
+    ids_copy.start()
+    ag_x0 = copy(5, w_hbm.at[0, :, part_rows[0]], w_all.at[k, y, x, z, :, part_rows[0]], to_x)
+    ag_y1 = copy(6, w_hbm.at[0, :, part_rows[1]], w_all.at[k, y, x, z, :, part_rows[1]], to_y)
+    ag_x0.start()
+    ag_y1.start()
+    ag_z = [copy(1 + d, w_hbm.at[0], w_all.at[k, y, x, z], to_z[d]) for d in range(n_z - 1)]
+    for c in ag_z:
+        c.start()
+
+    @pl.loop(0, 2 * rows, unroll=4)
     def _(i):
         at = pl.ds(pl.multiple_of(i * block, block), block)
         pltpu.make_async_copy(gate_hbm.at[:, at], gate.at[i], local.at[0]).start()
         pltpu.make_async_copy(up_hbm.at[:, at], up.at[i], local.at[1]).start()
 
-    barrier = pltpu.get_barrier_semaphore()
-    peers = [to_core, to_x, to_y] + to_z
-    for to in peers:
-        pl.semaphore_signal(barrier, inc=1, device_id=to, device_id_type=pl.DeviceIdType.MESH)
-    pl.semaphore_wait(barrier, len(peers))
-
-    ids_copy = copy(0, ids_vec, ids_in, to_y)
-    ids_copy.start()
-    ag_z = [copy(1 + d, w_hbm.at[0], w_all.at[k, y, x, z], to_z[d]) for d in range(n_z - 1)]
-    for c in ag_z:
+    own_w.wait()
+    ids_copy.wait_recv()
+    ids_local = pltpu.make_async_copy(ids_in, ids_other, local.at[4])
+    ids_local.start()
+    ids_local.wait()
+    ag_x0.wait_recv()
+    ag_zx = [same(23 + d, w_all.at[k, y, 1 - x, z, :, part_rows[0]], to_z[d]) for d in range(n_z - 1)]
+    ag_y1.wait_recv()
+    ag_zy = [
+        same(23 + n_z - 1 + d, w_all.at[k, 1 - y, x, z, :, part_rows[1]], to_z[d]) for d in range(n_z - 1)
+    ]
+    for c in ag_zx + ag_zy:
         c.start()
     for n, ref in enumerate((gate, up, cot)):
         pltpu.make_async_copy(ref, ref, local.at[n]).wait()
-    own_w.wait()
-
-    def partials(core, t, ids):
-        @pl.loop(0, 2 * n_z * cap, unroll=8)
+
+    def partials(core, t, xx, ids):
+        @pl.loop(0, n_z * cap, unroll=6)
         def _(i):
-            q, zz, xx = i % cap, i // cap % n_z, i // (cap * n_z)
+            q, zz = i % cap, i // cap
             slot = ids[0, (zz * 4 + xx * 2 + core) * cap + q]
             safe = lax.max(slot, 0)
             r = lax.div(safe, cols) + t * rows
             c = lax.rem(safe, cols)
             usable = lax.min(slot + 1, 1).astype(jnp.float32)
-            h = swiglu_value(gate[r], up[r])
+            h = hidden_value(gate[r], up[r])
             dy = cot[c]
             got = lax.dot_general(h, dy, (((0,), (0,)), ((), ())), preferred_element_type=jnp.float32)
             part[core, t, xx, zz, q] = (got * (usable * scale)).astype(part.dtype)
@@ -193,101 +219,132 @@
         total = dst[...].astype(jnp.float32) + src[...].astype(jnp.float32)
         dst[...] = total.astype(dst.dtype)
 
-    partials(1 - k, y, ids_ref)
-    core_p = [copy(13, part.at[1 - k, y], rc.at[y], to_core)]
-    core_p[0].start()
-    ids_copy.wait_recv()
-    ids_local = pltpu.make_async_copy(ids_in, ids_other, local.at[4])
-    ids_local.start()
-    ids_local.wait()
-    partials(1 - k, 1 - y, ids_other)
-    core_p.append(copy(14, part.at[1 - k, 1 - y], rc.at[1 - y], to_core))
-    core_p[1].start()
-    partials(k, y, ids_ref)
-    partials(k, 1 - y, ids_other)
+    quads = ((1 - y, 1 - x, ids_other), (y, 1 - x, ids_ref), (1 - y, x, ids_other), (y, x, ids_ref))
+    core_p = []
+
+    def send_core(n):
+        t, xx, ids = quads[n]
+        partials(1 - k, t, xx, ids)
+        core_p.append(copy(10 + n, part.at[1 - k, t, xx], rc.at[t, xx], to_core))
+        core_p[n].start()
+
+    def add_core(n):
+        t, xx, _ = quads[n]
+        core_p[n].wait_recv()
+
+        @pl.loop(0, n_z)
+        def _(i):
+            add(part.at[k, t, xx, i], rc.at[t, xx, i])
+
+    def own_core(n):
+        t, xx, ids = quads[n]
+        partials(k, t, xx, ids)
+
+    send_core(0)
+    own_core(0)
+    send_core(1)
+    add_core(0)
+    far = part.at[k, 1 - y, 1 - x]
+    rs_xa = copy(14, far.at[:, :, part_rows[0]], rx0.at[1 - y], to_x)
+    rs_ya = copy(15, far.at[:, :, part_rows[1]], ry1.at[1 - x], to_y)
+    rs_xa.start()
+    rs_ya.start()
+    own_core(1)
+    send_core(2)
+    add_core(1)
+    rs_xb = copy(16, part.at[k, y, 1 - x, :, :, part_rows[0]], rx0.at[y], to_x)
+    rs_xb.start()
+    own_core(2)
+    send_core(3)
+    add_core(2)
+    rs_yb = copy(17, part.at[k, 1 - y, x, :, :, part_rows[1]], ry1.at[x], to_y)
+    rs_yb.start()
+    own_core(3)
 
     for c in ag_z:
         c.wait_recv()
-    core_w = [same(4, w_all.at[k, y, x], to_core)]
-    ag_x0 = same(5, w_all.at[k, y, x, :, :, part_rows[0]], to_x)
-    ag_y1 = same(6, w_all.at[k, y, x, :, :, part_rows[1]], to_y)
-    ag_x0.start()
-    ag_y1.start()
+    mine = w_all.at[k, y, x]
+    ag_ya = same(4, mine.at[:, :, part_rows[0]], to_y)
+    ag_xa = same(7, mine.at[:, :, part_rows[1]], to_x)
+    ag_ya.start()
+    ag_xa.start()
+    core_w = [same(29, mine, to_core)]
     core_w[0].start()
-
-    for n, t in enumerate((y, 1 - y)):
-        core_p[n].wait_recv()
-
-        @pl.loop(0, 2 * n_z)
-        def _(i, t=t):
-            at = (t, i // n_z, i % n_z)
-            add(part.at[(k,) + at], rc.at[at])
-
-    rs_x0 = copy(15, part.at[k, :, 1 - x, :, :, part_rows[0]], rx0, to_x)
-    rs_y1 = copy(16, part.at[k, 1 - y, :, :, :, part_rows[1]], ry1, to_y)
-    rs_x0.start()
-    rs_y1.start()
-
-    ag_x0.wait_recv()
-    ag_y0 = same(9, w_all.at[k, y, :, :, :, part_rows[0]], to_y)
-    ag_y0.start()
-    core_w.append(same(7, w_all.at[k, y, 1 - x, :, :, part_rows[0]], to_core))
-    core_w[1].start()
-    ag_y1.wait_recv()
-    ag_x1 = same(10, w_all.at[k, :, x, :, :, part_rows[1]], to_x)
-    ag_x1.start()
-    core_w.append(same(8, w_all.at[k, 1 - y, x, :, :, part_rows[1]], to_core))
-    core_w[2].start()
+    add_core(3)
+
+    rs_xa.wait_recv()
+
+    @pl.loop(0, n_z)
+    def _(i):
+        add(part.at[k, 1 - y, x, i, :, part_rows[0]], rx0.at[1 - y, i])
+
+    rs_y0 = copy(18, part.at[k, 1 - y, x, :, :, part_rows[0]], ry0, to_y)
+    rs_y0.start()
+    rs_ya.wait_recv()
+
+    @pl.loop(0, n_z)
+    def _(i):
+        add(part.at[k, y, 1 - x, i, :, part_rows[1]], ry1.at[1 - x, i])
+
+    rs_x1 = copy(19, part.at[k, y, 1 - x, :, :, part_rows[1]], rx1, to_x)
+    rs_x1.start()
+
+    def to_core_w(ref):
+        core_w.append(same(29 + len(core_w), ref, to_core))
+        core_w[-1].start()
 
     contribs(k, y, x, ids_ref)
+    for c in ag_zx:
+        c.wait_recv()
+    ag_yb = same(8, w_all.at[k, y, 1 - x, :, :, part_rows[0]], to_y)
+    ag_yb.start()
+    to_core_w(w_all.at[k, y, 1 - x, :, :, part_rows[0]])
+    for c in ag_zy:
+        c.wait_recv()
+    ag_xb = same(9, w_all.at[k, 1 - y, x, :, :, part_rows[1]], to_x)
+    ag_xb.start()
+    to_core_w(w_all.at[k, 1 - y, x, :, :, part_rows[1]])
+
+    rs_z = []
+
+    def send_z(p, last, into, came, came_into):
+        last.wait_recv()
+        came.wait_recv()
+
+        @pl.loop(0, n_z)
+        def _(i):
+            ref = part.at[k, y, x, i, :, part_rows[p]]
+            total = ref[...].astype(jnp.float32) + into[i].astype(jnp.float32)
+            ref[...] = (total + came_into[i].astype(jnp.float32)).astype(ref.dtype)
+
+        for d in range(n_z - 1):
+            src = part.at[k, y, x, (z + d + 1) % n_z, :, part_rows[p]]
+            c = copy(37 + p * (n_z - 1) + d, src, rz.at[d, p], to_z[d])
+            c.start()
+            rs_z.append(c)
+
+    send_z(0, rs_xb, rx0.at[y], rs_y0, ry0)
+    send_z(1, rs_yb, ry1.at[x], rs_x1, rx1)
+
     core_w[0].wait_recv()
     contribs(1 - k, y, x, ids_ref)
-
-    rs_x0.wait_recv()
-
-    @pl.loop(0, 2 * n_z)
-    def _(i):
-        add(part.at[k, i // n_z, x, i % n_z, :, part_rows[0]], rx0.at[i // n_z, i % n_z])
-
-    rs_y0 = copy(17, part.at[k, 1 - y, x, :, :, part_rows[0]], ry0, to_y)
-    rs_y0.start()
-    rs_y1.wait_recv()
-
-    @pl.loop(0, 2 * n_z)
-    def _(i):
-        add(part.at[k, y, i // n_z, i % n_z, :, part_rows[1]], ry1.at[i // n_z, i % n_z])
-
-    rs_x1 = copy(18, part.at[k, y, 1 - x, :, :, part_rows[1]], rx1, to_x)
-    rs_x1.start()
-
-    ag_y0.wait_recv()
-    core_w.append(same(11, w_all.at[k, 1 - y, :, :, :, part_rows[0]], to_core))
-    core_w[3].start()
-    ag_x1.wait_recv()
-    core_w.append(same(12, w_all.at[k, :, 1 - x, :, :, part_rows[1]], to_core))
-    core_w[4].start()
-
-    rs_z = []
-    for p, came, into in ((0, rs_y0, ry0), (1, rs_x1, rx1)):
-        came.wait_recv()
-
-        @pl.loop(0, n_z)
-        def _(i, p=p, into=into):
-            add(part.at[k, y, x, i, :, part_rows[p]], into.at[i])
-
-        for d in range(n_z - 1):
-            c = copy(19 + p * (n_z - 1) + d, part.at[k, y, x, (z + d + 1) % n_z, :, part_rows[p]], rz.at[d, p], to_z[d])
-            c.start()
-            rs_z.append(c)
-
+    ag_ya.wait_recv()
+    to_core_w(w_all.at[k, 1 - y, x, :, :, part_rows[0]])
+    contribs(k, 1 - y, x, ids_other)
+    ag_xa.wait_recv()
+    to_core_w(w_all.at[k, y, 1 - x, :, :, part_rows[1]])
     contribs(k, y, 1 - x, ids_ref)
-    contribs(k, 1 - y, x, ids_other)
+    for c in (core_w[2], core_w[3]):
+        c.wait_recv()
+    contribs(1 - k, 1 - y, x, ids_other)
+    for c in (core_w[1], core_w[4]):
+        c.wait_recv()
+    contribs(1 - k, y, 1 - x, ids_ref)
+    ag_yb.wait_recv()
+    to_core_w(w_all.at[k, 1 - y, 1 - x, :, :, part_rows[0]])
+    ag_xb.wait_recv()
+    to_core_w(w_all.at[k, 1 - y, 1 - x, :, :, part_rows[1]])
     contribs(k, 1 - y, 1 - x, ids_other)
-    for c in core_w[1:]:
-        c.wait_recv()
-    contribs(1 - k, y, 1 - x, ids_ref)
-    contribs(1 - k, 1 - y, x, ids_other)
-    contribs(1 - k, 1 - y, 1 - x, ids_other)
 
     for c in rs_z:
         c.wait_recv()
@@ -296,7 +353,11 @@
         for d in range(n_z - 1):
             total = total + rz[d, p].astype(jnp.float32)
         wgrad_ref[0, :, part_rows[p]] = total
-    for c in [ids_copy, ag_x0, ag_y1, ag_y0, ag_x1, rs_x0, rs_y1, rs_y0, rs_x1] + ag_z + core_p + core_w + rs_z:
+    for c in core_w[5:]:
+        c.wait_recv()
+    contribs(1 - k, 1 - y, 1 - x, ids_other)
+    sent = [ids_copy, ag_x0, ag_y1, ag_xa, ag_ya, ag_xb, ag_yb, rs_xa, rs_ya, rs_xb, rs_yb, rs_x1, rs_y0]
+    for c in sent + ag_z + ag_zx + ag_zy + core_p + core_w + rs_z:
         c.wait_send()
 
 
@@ -304,7 +365,7 @@
     tokens, ff = gate.shape
     cap, block = w.shape[1:3]
     bf16 = jnp.bfloat16
-    any_spec = pl.BlockSpec(memory_space=pl.ANY)
+    any_spec = pl.BlockSpec(memory_space=pltpu.HBM)
     smem = pl.BlockSpec(memory_space=pltpu.SMEM)
     whole = pl.BlockSpec(memory_space=pltpu.VMEM)
     n_z = lax.axis_size("fsdp") // 4
@@ -332,8 +393,8 @@
             pltpu.VMEM((n_z, cap, half, block), bf16),
             pltpu.VMEM((n_z - 1, 2, cap, half, block), bf16),
             pltpu.SemaphoreType.DMA((5,)),
-            pltpu.SemaphoreType.DMA((19 + 2 * (n_z - 1),)),
-            pltpu.SemaphoreType.DMA((19 + 2 * (n_z - 1),)),
+            pltpu.SemaphoreType.DMA((37 + 2 * (n_z - 1),)),
+            pltpu.SemaphoreType.DMA((37 + 2 * (n_z - 1),)),
         ],
         compiler_params=pltpu.CompilerParams(
             collective_id=0, has_side_effects=True, vmem_limit_bytes=48 * MIB
@@ -362,14 +423,19 @@
                 at = (r // per, slice(None), pl.ds(pl.multiple_of(r % per * block, block), block))
                 dh_ref[at] += con_ref[f % 2, t, f // 2 % 2, f // 4, s % cap].astype(jnp.float32)
 
-    dh = dh_ref[step].astype(jnp.bfloat16)
-    dgate_ref[...], dup_ref[...] = swiglu_grads(dh, gate_ref[...], up_ref[...])
+    gate_f = gate_ref[...].astype(jnp.float32)
+    dh = dh_ref[step]
+    sig = sigmoid(gate_f)
+    silu = gate_f * sig
+    dup_ref[...] = (dh * silu).astype(dup_ref.dtype)
+    slope = sig + silu * (1.0 - sig)
+    dgate_ref[...] = (dh * up_ref[...].astype(jnp.float32) * slope).astype(dgate_ref.dtype)
 
 
 def local_grads(ids, other, contrib, cols, gate, up):
     tokens, ff = gate.shape
-    width = 1024
-    steps = ff // width
+    steps = 8
+    width = ff // steps
     smem = pl.BlockSpec(memory_space=pltpu.SMEM)
     tile = pl.BlockSpec((tokens, width), lambda i: (0, i))
     return pl.pallas_call(

time: 67.6 us -> 54.4 us (0.80)
  Pallas kernels: 62.4 us -> 49.2 us
    pallas_call x1, Pallas kernels: 51.5 us -> 40.4 us  [exchange(): pl.pallas_call(functools.partial(exchange_kernel, scale), out_shape=[jax....]
    pallas_call x1, Pallas kernels: 10.9 us -> 8.81 us  [local_grads(): pl.pallas_call(functools.partial(grads_kernel, cols), grid=(steps,), out_...]
where the time goes in v3:
time: 54.4 us; the launch traced here: 54.2 us
  Pallas kernels  49.2 us (90%)
  local copies, waits for them, and re-layouts  4.32 us (8%)
  between operations  0.68 us (1%)
    pallas_call x1, Pallas kernels, exchange(): pl.pallas_call(functools.partial(exchange_kernel, scale), out_shape=[jax....  40.4 us
    pallas_call x1, Pallas kernels, local_grads(): pl.pallas_call(functools.partial(grads_kernel, cols), grid=(steps,), out_...  8.81 us
    unnamed x11, local copies, waits for them, and re-layouts  4.32 us

profile of v3, /device:TPU:0, one launch (start us, length us, event | category | flops | bytes accessed | tf_op | source)
XLA Modules:
  0.0 54.2 jit_solution(17150225556523606481)
XLA Ops:
  0.6 0.0 copy-start.1
  0.6 0.0 copy-start
  0.7 0.0 copy-start.2
  0.7 1.5 %copy-done.2 = bf16[192,4096]{1,0:T(8,128)(2,1)S(1)} copy-done((bf16[192,4096]{1,0:T(8,128)(2,1)S(1)}, bf16[192,4096]{1,0:T(8,128)(2,1)}, u32[]{:S(2)}) %copy-start.2) | copy-done | bytes 1572888
  2.2 0.0 copy-start.3
  2.2 1.4 %copy-done.3 = bf16[1,3,128,128]{3,2,1,0:T(8,128)(2,1)S(1)} copy-done((bf16[1,3,128,128]{3,2,1,0:T(8,128)(2,1)S(1)}, bf16[1,3,128,128]{3,2,1,0:T(8,128)(2,1)}, u32[]{:S(2)}) %copy-start.3) | copy-done | bytes 98328
  3.6 0.0 copy-start.4
  3.6 0.7 %copy-done.4 = s32[1,48]{1,0:T(1,128)S(1)} copy-done((s32[1,48]{1,0:T(1,128)S(1)}, s32[1,48]{1,0:T(1,128)}, u32[]{:S(2)}) %copy-start.4) | copy-done | bytes 216
  4.3 40.4 %shard_map.76 = (s32[1,48]{1,0:T(1,128)S(1)}, bf16[2,2,2,4,3,96,128]{6,5,4,3,2,1,0:T(8,128)(2,1)S(1)}, f32[1,3,128,128]{3,2,1,0:T(8,128)S(1)}) custom-call(s32[1,48]{1,0:T(1,128)S(1)} %copy-done.4, s32[1,48]{1,0:T(1,128)S(1)} %copy-done.4, bf16[96,14336]{1,0:T(8,128)(2,1)} %gate_ref.1, bf16[96,14336]{1,0:T(8,128)(2,1)} %up_ref.1, ...), custom_call_target="tpu_custom_call" | custom-call | tf_op jit(solution)/shard_map/pallas_call | solution.py:373
  44.7 0.0 copy-done.1
  44.7 0.0 copy-done
  44.7 8.8 %shard_map.77 = (bf16[96,14336]{1,0:T(8,128)(2,1)}, bf16[96,14336]{1,0:T(8,128)(2,1)}) custom-call(s32[1,48]{1,0:T(1,128)S(1)} %copy-done.4, s32[1,48]{1,0:T(1,128)S(1)} %get-tuple-element.8.other_ref, bf16[2,2,2,4,3,96,128]{6,5,4,3,2,1,0:T(8,128)(2,1)S(1)} %get-tuple-element.9.con_ref, bf16[96,14336]{1,0:T(8,128)(2,1)S(1)} %copy-done, ...), custom_call_target="tpu_custom_call" | custom-call | tf_op jit(solution)/shard_map/pallas_call | solution.py:441
  53.5 0.7 %copy.9 = f32[1,3,128,128]{3,2,1,0:T(8,128)} copy(f32[1,3,128,128]{3,2,1,0:T(8,128)S(1)} %get-tuple-element.18) | data formatting | bytes 393216
Async XLA Ops:
  0.6 44.1 %copy-start.1 = (bf16[96,14336]{1,0:T(8,128)(2,1)S(1)}, bf16[96,14336]{1,0:T(8,128)(2,1)}, u32[]{:S(2)}) copy-start(bf16[96,14336]{1,0:T(8,128)(2,1)} %up_ref.1) | copy-start | bytes 8257540
  0.6 44.1 %copy-start = (bf16[96,14336]{1,0:T(8,128)(2,1)S(1)}, bf16[96,14336]{1,0:T(8,128)(2,1)}, u32[]{:S(2)}) copy-start(bf16[96,14336]{1,0:T(8,128)(2,1)} %gate_ref.1) | copy-start | bytes 8257540
  0.7 1.6 %copy-start.2 = (bf16[192,4096]{1,0:T(8,128)(2,1)S(1)}, bf16[192,4096]{1,0:T(8,128)(2,1)}, u32[]{:S(2)}) copy-start(bf16[192,4096]{1,0:T(8,128)(2,1)} %cot_hbm.1) | copy-start | bytes 4718596
  2.2 1.4 %copy-start.3 = (bf16[1,3,128,128]{3,2,1,0:T(8,128)(2,1)S(1)}, bf16[1,3,128,128]{3,2,1,0:T(8,128)(2,1)}, u32[]{:S(2)}) copy-start(bf16[1,3,128,128]{3,2,1,0:T(8,128)(2,1)} %w_hbm.1) | copy-start | bytes 294916
  3.6 0.7 %copy-start.4 = (s32[1,48]{1,0:T(1,128)S(1)}, s32[1,48]{1,0:T(1,128)}, u32[]{:S(2)}) copy-start(s32[1,48]{1,0:T(1,128)} %ids_ref.3) | copy-start | bytes 580

commit v4 on v3

--- a/solution.py
+++ b/solution.py
@@ -103,6 +103,13 @@
     return (d_gate, d_up, w_grad)
 
 
+def split_id(slot, cols):
+    safe = lax.max(slot, 0)
+    if cols & (cols - 1):
+        return lax.div(safe, cols), lax.rem(safe, cols)
+    return lax.shift_right_logical(safe, cols.bit_length() - 1), lax.bitwise_and(safe, cols - 1)
+
+
 def sigmoid(value):
     return 0.5 + 0.5 * jnp.tanh(0.5 * value)
 
@@ -114,8 +121,8 @@
 
 def exchange_kernel(
     scale, ids_ref, ids_vec, gate_hbm, up_hbm, cot_hbm, w_hbm,
-    ids_other, con_ref, wgrad_ref,
-    ids_in, gate, up, cot, w_all, part, rc, rx0, ry1, ry0, rx1, rz, local, send, recv,
+    ids_other, con_hbm, wgrad_ref,
+    con_ref, ids_in, gate, up, cot, w_all, part, rc, rx0, ry1, ry0, rx1, rz, local, send, recv,
 ):
     tokens = gate.shape[1]
     cap, block, _ = w_hbm.shape[1:]
@@ -152,6 +159,12 @@
         at = pl.ds(pl.multiple_of(i * block, block), block)
         pltpu.make_async_copy(cot_hbm.at[own_tokens, at], cot.at[i], local.at[2]).start()
 
+    @pl.loop(0, 2 * rows, unroll=4)
+    def _(i):
+        at = pl.ds(pl.multiple_of(i * block, block), block)
+        pltpu.make_async_copy(gate_hbm.at[:, at], gate.at[i], local.at[0]).start()
+        pltpu.make_async_copy(up_hbm.at[:, at], up.at[i], local.at[1]).start()
+
     own_w = pltpu.make_async_copy(w_hbm.at[0], w_all.at[k, y, x, z], local.at[3])
     own_w.start()
     pl.semaphore_wait(barrier, len(peers))
@@ -165,12 +178,6 @@
     ag_z = [copy(1 + d, w_hbm.at[0], w_all.at[k, y, x, z], to_z[d]) for d in range(n_z - 1)]
     for c in ag_z:
         c.start()
-
-    @pl.loop(0, 2 * rows, unroll=4)
-    def _(i):
-        at = pl.ds(pl.multiple_of(i * block, block), block)
-        pltpu.make_async_copy(gate_hbm.at[:, at], gate.at[i], local.at[0]).start()
-        pltpu.make_async_copy(up_hbm.at[:, at], up.at[i], local.at[1]).start()
 
     own_w.wait()
     ids_copy.wait_recv()
@@ -188,32 +195,38 @@
     for n, ref in enumerate((gate, up, cot)):
         pltpu.make_async_copy(ref, ref, local.at[n]).wait()
 
+    def slots_of(core, xx, ids):
+        def visit(step):
+            @pl.loop(0, n_z, unroll=2)
+            def _(zz):
+                first = ((zz * 2 + xx) * 2 + core) * cap
+                for q in range(cap):
+                    slot = ids[0, first + q]
+                    r, c = split_id(slot, cols)
+                    step(zz, q, r, c, lax.min(slot + 1, 1).astype(jnp.float32))
+
+        return visit
+
     def partials(core, t, xx, ids):
-        @pl.loop(0, n_z * cap, unroll=6)
-        def _(i):
-            q, zz = i % cap, i // cap
-            slot = ids[0, (zz * 4 + xx * 2 + core) * cap + q]
-            safe = lax.max(slot, 0)
-            r = lax.div(safe, cols) + t * rows
-            c = lax.rem(safe, cols)
-            usable = lax.min(slot + 1, 1).astype(jnp.float32)
-            h = hidden_value(gate[r], up[r])
-            dy = cot[c]
-            got = lax.dot_general(h, dy, (((0,), (0,)), ((), ())), preferred_element_type=jnp.float32)
+        @slots_of(core, xx, ids)
+        def _(zz, q, r, c, usable):
+            h = hidden_value(gate[r + t * rows], up[r + t * rows])
+            got = lax.dot_general(h, cot[c], (((0,), (0,)), ((), ())), preferred_element_type=jnp.float32)
             part[core, t, xx, zz, q] = (got * (usable * scale)).astype(part.dtype)
 
+    con_out = []
+
     def contribs(core, t, xx, ids):
-        @pl.loop(0, n_z * cap, unroll=6)
-        def _(i):
-            q, zz = i % cap, i // cap
-            slot = ids[0, (zz * 4 + xx * 2 + core) * cap + q]
-            c = lax.rem(lax.max(slot, 0), cols)
-            usable = lax.min(slot + 1, 1).astype(jnp.float32)
+        @slots_of(core, xx, ids)
+        def _(zz, q, r, c, usable):
             got = lax.dot_general(
-                cot[c], w_all[core, t, xx, zz, q], (((1,), (1,)), ((), ())),
-                preferred_element_type=jnp.float32,
+                cot[c], w_all[core, t, xx, zz, q], (((1,), (1,)), ((), ())), preferred_element_type=jnp.float32
             )
             con_ref[core, t, xx, zz, q] = (got * usable).astype(con_ref.dtype)
+
+        out = pltpu.make_async_copy(con_ref.at[core, t, xx], con_hbm.at[core, t, xx], local.at[5 + len(con_out)])
+        out.start()
+        con_out.append(out)
 
     def add(dst, src):
         total = dst[...].astype(jnp.float32) + src[...].astype(jnp.float32)
@@ -261,6 +274,25 @@
     rs_yb.start()
     own_core(3)
 
+    add_core(3)
+
+    rs_xa.wait_recv()
+
+    @pl.loop(0, n_z)
+    def _(i):
+        add(part.at[k, 1 - y, x, i, :, part_rows[0]], rx0.at[1 - y, i])
+
+    rs_y0 = copy(18, part.at[k, 1 - y, x, :, :, part_rows[0]], ry0, to_y)
+    rs_y0.start()
+    rs_ya.wait_recv()
+
+    @pl.loop(0, n_z)
+    def _(i):
+        add(part.at[k, y, 1 - x, i, :, part_rows[1]], ry1.at[1 - x, i])
+
+    rs_x1 = copy(19, part.at[k, y, 1 - x, :, :, part_rows[1]], rx1, to_x)
+    rs_x1.start()
+
     for c in ag_z:
         c.wait_recv()
     mine = w_all.at[k, y, x]
@@ -270,24 +302,6 @@
     ag_xa.start()
     core_w = [same(29, mine, to_core)]
     core_w[0].start()
-    add_core(3)
-
-    rs_xa.wait_recv()
-
-    @pl.loop(0, n_z)
-    def _(i):
-        add(part.at[k, 1 - y, x, i, :, part_rows[0]], rx0.at[1 - y, i])
-
-    rs_y0 = copy(18, part.at[k, 1 - y, x, :, :, part_rows[0]], ry0, to_y)
-    rs_y0.start()
-    rs_ya.wait_recv()
-
-    @pl.loop(0, n_z)
-    def _(i):
-        add(part.at[k, y, 1 - x, i, :, part_rows[1]], ry1.at[1 - x, i])
-
-    rs_x1 = copy(19, part.at[k, y, 1 - x, :, :, part_rows[1]], rx1, to_x)
-    rs_x1.start()
 
     def to_core_w(ref):
         core_w.append(same(29 + len(core_w), ref, to_core))
@@ -359,6 +373,8 @@
     sent = [ids_copy, ag_x0, ag_y1, ag_xa, ag_ya, ag_xb, ag_yb, rs_xa, rs_ya, rs_xb, rs_yb, rs_x1, rs_y0]
     for c in sent + ag_z + ag_zx + ag_zy + core_p + core_w + rs_z:
         c.wait_send()
+    for c in con_out:
+        c.wait()
 
 
 def exchange(gate, up, cot, w, ids, scale):
@@ -377,9 +393,10 @@
             jax.ShapeDtypeStruct((2, 2, 2, n_z, cap, tokens, block), bf16),
             jax.ShapeDtypeStruct(w.shape, jnp.float32),
         ],
-        in_specs=[smem, whole, any_spec, any_spec, any_spec, any_spec],
-        out_specs=[smem, whole, whole],
+        in_specs=[smem, any_spec, any_spec, any_spec, any_spec, any_spec],
+        out_specs=[smem, any_spec, whole],
         scratch_shapes=[
+            pltpu.VMEM((2, 2, 2, n_z, cap, tokens, block), bf16),
             pltpu.VMEM(ids.shape, ids.dtype),
             pltpu.VMEM((ff // block, tokens, block), bf16),
             pltpu.VMEM((ff // block, tokens, block), bf16),
@@ -392,69 +409,84 @@
             pltpu.VMEM((n_z, cap, half, block), bf16),
             pltpu.VMEM((n_z, cap, half, block), bf16),
             pltpu.VMEM((n_z - 1, 2, cap, half, block), bf16),
-            pltpu.SemaphoreType.DMA((5,)),
+            pltpu.SemaphoreType.DMA((13,)),
             pltpu.SemaphoreType.DMA((37 + 2 * (n_z - 1),)),
             pltpu.SemaphoreType.DMA((37 + 2 * (n_z - 1),)),
         ],
         compiler_params=pltpu.CompilerParams(
-            collective_id=0, has_side_effects=True, vmem_limit_bytes=48 * MIB
+            collective_id=0, has_side_effects=True, vmem_limit_bytes=60 * MIB
         ),
     )(ids, ids, gate, up, cot, w)
 
 
-def grads_kernel(cols, ids_ref, other_ref, con_ref, gate_ref, up_ref, dgate_ref, dup_ref, dh_ref):
-    n_z, cap, tokens, block = con_ref.shape[3:]
-    steps, _, width = dh_ref.shape
-    per = width // block
-    rows = steps * per // 2
+def grads_kernel(
+    cols, ids_ref, other_ref, con_hbm, wgrad_in, gate_ref, up_ref,
+    dgate_ref, dup_ref, wgrad_out, dh_ref, con_ref, con_sem, wgrad_sem,
+):
+    n_z, cap, _, block = con_ref.shape[3:]
+    blocks = dh_ref.shape[0]
+    per = gate_ref.shape[1] // block
     y = lax.axis_index("tensor")
     step = pl.program_id(0)
 
     @pl.when(step == 0)
     def _():
+        con_copy = pltpu.make_async_copy(con_hbm, con_ref, con_sem)
+        con_copy.start()
+        pltpu.make_async_copy(wgrad_in, wgrad_out, wgrad_sem).start()
         dh_ref[...] = jnp.zeros_like(dh_ref)
+        con_copy.wait()
         for t, ids in ((y, ids_ref), (1 - y, other_ref)):
-
-            @pl.loop(0, 4 * n_z * cap, unroll=4)
-            def _(s, t=t, ids=ids):
-                slot = ids[0, s]
+            for s in range(4 * n_z * cap):
                 f = s // cap
-                r = jnp.maximum(slot, 0) // cols + t * rows
-                at = (r // per, slice(None), pl.ds(pl.multiple_of(r % per * block, block), block))
-                dh_ref[at] += con_ref[f % 2, t, f // 2 % 2, f // 4, s % cap].astype(jnp.float32)
-
-    gate_f = gate_ref[...].astype(jnp.float32)
-    dh = dh_ref[step]
-    sig = sigmoid(gate_f)
-    silu = gate_f * sig
-    dup_ref[...] = (dh * silu).astype(dup_ref.dtype)
-    slope = sig + silu * (1.0 - sig)
-    dgate_ref[...] = (dh * up_ref[...].astype(jnp.float32) * slope).astype(dgate_ref.dtype)
-
-
-def local_grads(ids, other, contrib, cols, gate, up):
+                r = split_id(ids[0, s], cols)[0] + t * (blocks // 2)
+                dh_ref[r] += con_ref[f % 2, t, f // 2 % 2, f // 4, s % cap].astype(jnp.float32)
+
+    for j in range(per):
+        at = slice(j * block, (j + 1) * block)
+        gate_f = gate_ref[:, at].astype(jnp.float32)
+        dh = dh_ref[step * per + j]
+        sig = sigmoid(gate_f)
+        silu = gate_f * sig
+        dup_ref[:, at] = (dh * silu).astype(dup_ref.dtype)
+        slope = sig + silu * (1.0 - sig)
+        dgate_ref[:, at] = (dh * up_ref[:, at].astype(jnp.float32) * slope).astype(dgate_ref.dtype)
+
+    @pl.when(step == pl.num_programs(0) - 1)
+    def _():
+        pltpu.make_async_copy(wgrad_in, wgrad_out, wgrad_sem).wait()
+
+
+def local_grads(ids, other, contrib, w_grad, cols, gate, up):
     tokens, ff = gate.shape
     steps = 8
     width = ff // steps
+    block = contrib.shape[-1]
     smem = pl.BlockSpec(memory_space=pltpu.SMEM)
+    hbm = pl.BlockSpec(memory_space=pltpu.HBM)
     tile = pl.BlockSpec((tokens, width), lambda i: (0, i))
     return pl.pallas_call(
         functools.partial(grads_kernel, cols),
         grid=(steps,),
-        out_shape=[jax.ShapeDtypeStruct(gate.shape, jnp.bfloat16)] * 2,
-        in_specs=[smem, smem, pl.BlockSpec(memory_space=pltpu.VMEM), tile, tile],
-        out_specs=[tile, tile],
-        scratch_shapes=[pltpu.VMEM((steps, tokens, width), jnp.float32)],
-        compiler_params=pltpu.CompilerParams(vmem_limit_bytes=40 * MIB),
-    )(ids, other, contrib, gate, up)
+        out_shape=[jax.ShapeDtypeStruct(gate.shape, jnp.bfloat16)] * 2
+        + [jax.ShapeDtypeStruct(w_grad.shape, w_grad.dtype)],
+        in_specs=[smem, smem, hbm, hbm, tile, tile],
+        out_specs=[tile, tile, hbm],
+        scratch_shapes=[
+            pltpu.VMEM((ff // block, tokens, block), jnp.float32),
+            pltpu.VMEM(contrib.shape, contrib.dtype),
+            pltpu.SemaphoreType.DMA,
+            pltpu.SemaphoreType.DMA,
+        ],
+        compiler_params=pltpu.CompilerParams(vmem_limit_bytes=60 * MIB),
+    )(ids, other, contrib, w_grad, gate, up)
 
 
 def body(gate_pre, up_pre, cotangent, w_slots, slot_ids):
     scale = 1.0 / math.sqrt(cotangent.shape[0] * lax.axis_size("fsdp"))
     other, contrib, w_grad = exchange(gate_pre, up_pre, cotangent, w_slots, slot_ids, scale)
     cols = cotangent.shape[1] // w_slots.shape[2]
-    d_gate, d_up = local_grads(slot_ids, other, contrib, cols, gate_pre, up_pre)
-    return (d_gate, d_up, w_grad)
+    return tuple(local_grads(slot_ids, other, contrib, w_grad, cols, gate_pre, up_pre))
 
 
 def solution(mesh):

time: 54.4 us -> 51.2 us (0.941)
  local copies, waits for them, and re-layouts: 4.32 us -> 0 us
  Pallas kernels: 49.2 us -> 50.2 us
    unnamed x11 -> x0, local copies, waits for them, and re-layouts: 4.32 us -> none
    pallas_call x1, Pallas kernels: 8.81 us -> 10.8 us  [local_grads(): pl.pallas_call(functools.partial(grads_kernel, cols), grid=(steps,), out_...]
    pallas_call x1, Pallas kernels: 40.4 us -> 39.4 us  [exchange(): pl.pallas_call(functools.partial(exchange_kernel, scale), out_shape=[jax....]
where the time goes in v4:
time: 51.2 us; the launch traced here: 50.9 us
  Pallas kernels  50.2 us (98%)
  between operations  0.64 us (1%)
    pallas_call x1, Pallas kernels, exchange(): pl.pallas_call(functools.partial(exchange_kernel, scale), out_shape=[jax....  39.4 us
    pallas_call x1, Pallas kernels, local_grads(): pl.pallas_call(functools.partial(grads_kernel, cols), grid=(steps,), out_...  10.8 us

profile of v4, /device:TPU:0, one launch (start us, length us, event | category | flops | bytes accessed | tf_op | source)
XLA Modules:
  0.0 50.9 jit_solution(1334524270080050202)
XLA Ops:
  0.6 39.4 %shard_map.76 = (s32[1,48]{1,0:T(1,128)}, bf16[2,2,2,4,3,96,128]{6,5,4,3,2,1,0:T(8,128)(2,1)}, f32[1,3,128,128]{3,2,1,0:T(8,128)}) custom-call(s32[1,48]{1,0:T(1,128)} %ids_ref.3, s32[1,48]{1,0:T(1,128)} %ids_ref.3, bf16[96,14336]{1,0:T(8,128)(2,1)} %gate_ref.1, bf16[96,14336]{1,0:T(8,128)(2,1)} %up_ref.1, bf16[192,4096]{1,0:T(8,128)(2,1)} %cot_hbm.1, ...), custom_call_target="tpu_custom_call" | custom-call | tf_op jit(solution)/shard_map/pallas_call | solution.py:389
  40.1 10.8 %shard_map.77 = (bf16[96,14336]{1,0:T(8,128)(2,1)}, bf16[96,14336]{1,0:T(8,128)(2,1)}, f32[1,3,128,128]{3,2,1,0:T(8,128)}) custom-call(s32[1,48]{1,0:T(1,128)} %ids_ref.3, s32[1,48]{1,0:T(1,128)} %get-tuple-element.6.other_ref, bf16[2,2,2,4,3,96,128]{6,5,4,3,2,1,0:T(8,128)(2,1)} %get-tuple-element.7.con_hbm, f32[1,3,128,128]{3,2,1,0:T(8,128)} %get-tuple-element.8.wgrad_in, ...), custom_call_target="tpu_custom_call" | custom-call | tf_op jit(solution)/shard_map/pallas_call | solution.py:468

commit v5 on v4

--- a/solution.py
+++ b/solution.py
@@ -171,8 +171,8 @@
 
     ids_copy = copy(0, ids_vec, ids_in, to_y)
     ids_copy.start()
-    ag_x0 = copy(5, w_hbm.at[0, :, part_rows[0]], w_all.at[k, y, x, z, :, part_rows[0]], to_x)
-    ag_y1 = copy(6, w_hbm.at[0, :, part_rows[1]], w_all.at[k, y, x, z, :, part_rows[1]], to_y)
+    ag_x0 = copy(5, w_hbm.at[0], w_all.at[k, y, x, z], to_x)
+    ag_y1 = copy(6, w_hbm.at[0], w_all.at[k, y, x, z], to_y)
     ag_x0.start()
     ag_y1.start()
     ag_z = [copy(1 + d, w_hbm.at[0], w_all.at[k, y, x, z], to_z[d]) for d in range(n_z - 1)]
@@ -184,14 +184,6 @@
     ids_local = pltpu.make_async_copy(ids_in, ids_other, local.at[4])
     ids_local.start()
     ids_local.wait()
-    ag_x0.wait_recv()
-    ag_zx = [same(23 + d, w_all.at[k, y, 1 - x, z, :, part_rows[0]], to_z[d]) for d in range(n_z - 1)]
-    ag_y1.wait_recv()
-    ag_zy = [
-        same(23 + n_z - 1 + d, w_all.at[k, 1 - y, x, z, :, part_rows[1]], to_z[d]) for d in range(n_z - 1)
-    ]
-    for c in ag_zx + ag_zy:
-        c.start()
     for n, ref in enumerate((gate, up, cot)):
         pltpu.make_async_copy(ref, ref, local.at[n]).wait()
 
@@ -254,14 +246,22 @@
         partials(k, t, xx, ids)
 
     send_core(0)
+    ag_x0.wait_recv()
+    ag_zx = [same(23 + d, w_all.at[k, y, 1 - x, z, :, part_rows[0]], to_z[d]) for d in range(n_z - 1)]
+    ag_y1.wait_recv()
+    ag_zy = [
+        same(23 + n_z - 1 + d, w_all.at[k, 1 - y, x, z, :, part_rows[1]], to_z[d]) for d in range(n_z - 1)
+    ]
+    for c in ag_zx + ag_zy:
+        c.start()
     own_core(0)
-    send_core(1)
     add_core(0)
     far = part.at[k, 1 - y, 1 - x]
     rs_xa = copy(14, far.at[:, :, part_rows[0]], rx0.at[1 - y], to_x)
     rs_ya = copy(15, far.at[:, :, part_rows[1]], ry1.at[1 - x], to_y)
     rs_xa.start()
     rs_ya.start()
+    send_core(1)
     own_core(1)
     send_core(2)
     add_core(1)
@@ -296,10 +296,13 @@
     for c in ag_z:
         c.wait_recv()
     mine = w_all.at[k, y, x]
-    ag_ya = same(4, mine.at[:, :, part_rows[0]], to_y)
-    ag_xa = same(7, mine.at[:, :, part_rows[1]], to_x)
-    ag_ya.start()
-    ag_xa.start()
+    ag_ya, ag_xa = [], []
+    for d in range(n_z - 1):
+        came = mine.at[(z + d + 1) % n_z]
+        ag_ya.append(same(37 + 2 * (n_z - 1) + d, came.at[:, part_rows[0]], to_y))
+        ag_xa.append(same(37 + 3 * (n_z - 1) + d, came.at[:, part_rows[1]], to_x))
+        ag_ya[d].start()
+        ag_xa[d].start()
     core_w = [same(29, mine, to_core)]
     core_w[0].start()
 
@@ -342,10 +345,12 @@
 
     core_w[0].wait_recv()
     contribs(1 - k, y, x, ids_ref)
-    ag_ya.wait_recv()
+    for c in ag_ya:
+        c.wait_recv()
     to_core_w(w_all.at[k, 1 - y, x, :, :, part_rows[0]])
     contribs(k, 1 - y, x, ids_other)
-    ag_xa.wait_recv()
+    for c in ag_xa:
+        c.wait_recv()
     to_core_w(w_all.at[k, y, 1 - x, :, :, part_rows[1]])
     contribs(k, y, 1 - x, ids_ref)
     for c in (core_w[2], core_w[3]):
@@ -370,8 +375,8 @@
     for c in core_w[5:]:
         c.wait_recv()
     contribs(1 - k, 1 - y, 1 - x, ids_other)
-    sent = [ids_copy, ag_x0, ag_y1, ag_xa, ag_ya, ag_xb, ag_yb, rs_xa, rs_ya, rs_xb, rs_yb, rs_x1, rs_y0]
-    for c in sent + ag_z + ag_zx + ag_zy + core_p + core_w + rs_z:
+    sent = [ids_copy, ag_x0, ag_y1, ag_xb, ag_yb, rs_xa, rs_ya, rs_xb, rs_yb, rs_x1, rs_y0]
+    for c in sent + ag_z + ag_xa + ag_ya + ag_zx + ag_zy + core_p + core_w + rs_z:
         c.wait_send()
     for c in con_out:
         c.wait()
@@ -410,8 +415,8 @@
             pltpu.VMEM((n_z, cap, half, block), bf16),
             pltpu.VMEM((n_z - 1, 2, cap, half, block), bf16),
             pltpu.SemaphoreType.DMA((13,)),
-            pltpu.SemaphoreType.DMA((37 + 2 * (n_z - 1),)),
-            pltpu.SemaphoreType.DMA((37 + 2 * (n_z - 1),)),
+            pltpu.SemaphoreType.DMA((37 + 4 * (n_z - 1),)),
+            pltpu.SemaphoreType.DMA((37 + 4 * (n_z - 1),)),
         ],
         compiler_params=pltpu.CompilerParams(
             collective_id=0, has_side_effects=True, vmem_limit_bytes=60 * MIB
@@ -421,10 +426,9 @@
 
 def grads_kernel(
     cols, ids_ref, other_ref, con_hbm, wgrad_in, gate_ref, up_ref,
-    dgate_ref, dup_ref, wgrad_out, dh_ref, con_ref, con_sem, wgrad_sem,
+    dgate_ref, dup_ref, wgrad_out, dh_own, dh_other, con_ref, con_sem, wgrad_sem,
 ):
     n_z, cap, _, block = con_ref.shape[3:]
-    blocks = dh_ref.shape[0]
     per = gate_ref.shape[1] // block
     y = lax.axis_index("tensor")
     step = pl.program_id(0)
@@ -434,23 +438,36 @@
         con_copy = pltpu.make_async_copy(con_hbm, con_ref, con_sem)
         con_copy.start()
         pltpu.make_async_copy(wgrad_in, wgrad_out, wgrad_sem).start()
-        dh_ref[...] = jnp.zeros_like(dh_ref)
+        dh_own[...] = jnp.zeros_like(dh_own)
+        dh_other[...] = jnp.zeros_like(dh_other)
         con_copy.wait()
-        for t, ids in ((y, ids_ref), (1 - y, other_ref)):
-            for s in range(4 * n_z * cap):
-                f = s // cap
-                r = split_id(ids[0, s], cols)[0] + t * (blocks // 2)
+        for s in range(4 * n_z * cap):
+            f = s // cap
+            for t, ids, dh_ref in ((y, ids_ref, dh_own), (1 - y, other_ref, dh_other)):
+                r = split_id(ids[0, s], cols)[0]
                 dh_ref[r] += con_ref[f % 2, t, f // 2 % 2, f // 4, s % cap].astype(jnp.float32)
 
-    for j in range(per):
-        at = slice(j * block, (j + 1) * block)
-        gate_f = gate_ref[:, at].astype(jnp.float32)
-        dh = dh_ref[step * per + j]
-        sig = sigmoid(gate_f)
-        silu = gate_f * sig
-        dup_ref[:, at] = (dh * silu).astype(dup_ref.dtype)
-        slope = sig + silu * (1.0 - sig)
-        dgate_ref[:, at] = (dh * up_ref[:, at].astype(jnp.float32) * slope).astype(dgate_ref.dtype)
+    def apply(first, dh_ref):
+        for j in range(per):
+            at = slice(j * block, (j + 1) * block)
+            gate_f = gate_ref[:, at].astype(jnp.float32)
+            dh = dh_ref[first + j]
+            sig = sigmoid(gate_f)
+            silu = gate_f * sig
+            dup_ref[:, at] = (dh * silu).astype(dup_ref.dtype)
+            slope = sig + silu * (1.0 - sig)
+            dgate_ref[:, at] = (dh * up_ref[:, at].astype(jnp.float32) * slope).astype(dgate_ref.dtype)
+
+    half_steps = pl.num_programs(0) // 2
+    first = step % half_steps * per
+
+    @pl.when(step // half_steps == y)
+    def _():
+        apply(first, dh_own)
+
+    @pl.when(step // half_steps != y)
+    def _():
+        apply(first, dh_other)
 
     @pl.when(step == pl.num_programs(0) - 1)
     def _():
@@ -473,7 +490,8 @@
         in_specs=[smem, smem, hbm, hbm, tile, tile],
         out_specs=[tile, tile, hbm],
         scratch_shapes=[
-            pltpu.VMEM((ff // block, tokens, block), jnp.float32),
+            pltpu.VMEM((ff // block // 2, tokens, block), jnp.float32),
+            pltpu.VMEM((ff // block // 2, tokens, block), jnp.float32),
             pltpu.VMEM(contrib.shape, contrib.dtype),
             pltpu.SemaphoreType.DMA,
             pltpu.SemaphoreType.DMA,

time: 51.2 us -> 49.7 us (0.971)
  Pallas kernels: 50.2 us -> 48.7 us
    pallas_call x1, Pallas kernels: 39.4 us -> 38.2 us  [exchange(): pl.pallas_call(functools.partial(exchange_kernel, scale), out_shape=[jax....]
where the time goes in v5:
time: 49.7 us; the launch traced here: 49.3 us
  Pallas kernels  48.7 us (98%)
  between operations  0.64 us (1%)
    pallas_call x1, Pallas kernels, exchange(): pl.pallas_call(functools.partial(exchange_kernel, scale), out_shape=[jax....  38.2 us
    pallas_call x1, Pallas kernels, local_grads(): pl.pallas_call(functools.partial(grads_kernel, cols), grid=(steps,), out_...  10.4 us

profile of v5, /device:TPU:0, one launch (start us, length us, event | category | flops | bytes accessed | tf_op | source)
XLA Modules:
  0.0 49.3 jit_solution(8674042755342592891)
XLA Ops:
  0.6 38.2 %shard_map.76 = (s32[1,48]{1,0:T(1,128)}, bf16[2,2,2,4,3,96,128]{6,5,4,3,2,1,0:T(8,128)(2,1)}, f32[1,3,128,128]{3,2,1,0:T(8,128)}) custom-call(s32[1,48]{1,0:T(1,128)} %ids_ref.3, s32[1,48]{1,0:T(1,128)} %ids_ref.3, bf16[96,14336]{1,0:T(8,128)(2,1)} %gate_ref.1, bf16[96,14336]{1,0:T(8,128)(2,1)} %up_ref.1, bf16[192,4096]{1,0:T(8,128)(2,1)} %cot_hbm.1, ...), custom_call_target="tpu_custom_call" | custom-call | tf_op jit(solution)/shard_map/pallas_call | solution.py:394
  38.9 10.4 %shard_map.77 = (bf16[96,14336]{1,0:T(8,128)(2,1)}, bf16[96,14336]{1,0:T(8,128)(2,1)}, f32[1,3,128,128]{3,2,1,0:T(8,128)}) custom-call(s32[1,48]{1,0:T(1,128)} %ids_ref.3, s32[1,48]{1,0:T(1,128)} %get-tuple-element.6.other_ref, bf16[2,2,2,4,3,96,128]{6,5,4,3,2,1,0:T(8,128)(2,1)} %get-tuple-element.7.con_hbm, f32[1,3,128,128]{3,2,1,0:T(8,128)} %get-tuple-element.8.wgrad_in, ...), custom_call_target="tpu_custom_call" | custom-call | tf_op jit(solution)/shard_map/pallas_call | solution.py:485

commit v6 on v5

--- a/solution.py
+++ b/solution.py
@@ -425,11 +425,12 @@
 
 
 def grads_kernel(
-    cols, ids_ref, other_ref, con_hbm, wgrad_in, gate_ref, up_ref,
-    dgate_ref, dup_ref, wgrad_out, dh_own, dh_other, con_ref, con_sem, wgrad_sem,
+    cols, ids_ref, other_ref, con_hbm, wgrad_in, gate_hbm, up_hbm,
+    dgate_ref, dup_ref, wgrad_out, dh_own, dh_other, con_ref, gate_ref, up_ref,
+    con_sem, wgrad_sem, gate_sem, up_sem,
 ):
     n_z, cap, _, block = con_ref.shape[3:]
-    per = gate_ref.shape[1] // block
+    per = dgate_ref.shape[1] // block
     y = lax.axis_index("tensor")
     step = pl.program_id(0)
 
@@ -437,6 +438,10 @@
     def _():
         con_copy = pltpu.make_async_copy(con_hbm, con_ref, con_sem)
         con_copy.start()
+        gate_copy = pltpu.make_async_copy(gate_hbm, gate_ref, gate_sem)
+        gate_copy.start()
+        up_copy = pltpu.make_async_copy(up_hbm, up_ref, up_sem)
+        up_copy.start()
         pltpu.make_async_copy(wgrad_in, wgrad_out, wgrad_sem).start()
         dh_own[...] = jnp.zeros_like(dh_own)
         dh_other[...] = jnp.zeros_like(dh_other)
@@ -446,17 +451,20 @@
             for t, ids, dh_ref in ((y, ids_ref, dh_own), (1 - y, other_ref, dh_other)):
                 r = split_id(ids[0, s], cols)[0]
                 dh_ref[r] += con_ref[f % 2, t, f // 2 % 2, f // 4, s % cap].astype(jnp.float32)
+        gate_copy.wait()
+        up_copy.wait()
 
     def apply(first, dh_ref):
         for j in range(per):
             at = slice(j * block, (j + 1) * block)
-            gate_f = gate_ref[:, at].astype(jnp.float32)
+            here = pl.ds(pl.multiple_of((step * per + j) * block, block), block)
+            gate_f = gate_ref[:, here].astype(jnp.float32)
             dh = dh_ref[first + j]
             sig = sigmoid(gate_f)
             silu = gate_f * sig
             dup_ref[:, at] = (dh * silu).astype(dup_ref.dtype)
             slope = sig + silu * (1.0 - sig)
-            dgate_ref[:, at] = (dh * up_ref[:, at].astype(jnp.float32) * slope).astype(dgate_ref.dtype)
+            dgate_ref[:, at] = (dh * up_ref[:, here].astype(jnp.float32) * slope).astype(dgate_ref.dtype)
 
     half_steps = pl.num_programs(0) // 2
     first = step % half_steps * per
@@ -487,12 +495,16 @@
         grid=(steps,),
         out_shape=[jax.ShapeDtypeStruct(gate.shape, jnp.bfloat16)] * 2
         + [jax.ShapeDtypeStruct(w_grad.shape, w_grad.dtype)],
-        in_specs=[smem, smem, hbm, hbm, tile, tile],
+        in_specs=[smem, smem, hbm, hbm, hbm, hbm],
         out_specs=[tile, tile, hbm],
         scratch_shapes=[
             pltpu.VMEM((ff // block // 2, tokens, block), jnp.float32),
             pltpu.VMEM((ff // block // 2, tokens, block), jnp.float32),
             pltpu.VMEM(contrib.shape, contrib.dtype),
+            pltpu.VMEM(gate.shape, gate.dtype),
+            pltpu.VMEM(up.shape, up.dtype),
+            pltpu.SemaphoreType.DMA,
+            pltpu.SemaphoreType.DMA,
             pltpu.SemaphoreType.DMA,
             pltpu.SemaphoreType.DMA,
         ],

time: 49.7 us -> 48.4 us (0.974)
  Pallas kernels: 48.7 us -> 47.6 us
    pallas_call x1, Pallas kernels: 10.4 us -> 9.36 us  [local_grads(): pl.pallas_call(functools.partial(grads_kernel, cols), grid=(steps,), out_...]
where the time goes in v6:
time: 48.4 us; the launch traced here: 48.2 us
  Pallas kernels  47.6 us (98%)
  between operations  0.64 us (1%)
    pallas_call x1, Pallas kernels, exchange(): pl.pallas_call(functools.partial(exchange_kernel, scale), out_shape=[jax....  38.2 us
    pallas_call x1, Pallas kernels, local_grads(): pl.pallas_call(functools.partial(grads_kernel, cols), grid=(steps,), out_...  9.36 us

profile of v6, /device:TPU:0, one launch (start us, length us, event | category | flops | bytes accessed | tf_op | source)
XLA Modules:
  0.0 48.2 jit_solution(6651577379109002723)
XLA Ops:
  0.6 38.2 %shard_map.76 = (s32[1,48]{1,0:T(1,128)}, bf16[2,2,2,4,3,96,128]{6,5,4,3,2,1,0:T(8,128)(2,1)}, f32[1,3,128,128]{3,2,1,0:T(8,128)}) custom-call(s32[1,48]{1,0:T(1,128)} %ids_ref.3, s32[1,48]{1,0:T(1,128)} %ids_ref.3, bf16[96,14336]{1,0:T(8,128)(2,1)} %gate_hbm.3, bf16[96,14336]{1,0:T(8,128)(2,1)} %up_hbm.3, bf16[192,4096]{1,0:T(8,128)(2,1)} %cot_hbm.1, ...), custom_call_target="tpu_custom_call" | custom-call | tf_op jit(solution)/shard_map/pallas_call | solution.py:394
  38.9 9.4 %shard_map.77 = (bf16[96,14336]{1,0:T(8,128)(2,1)}, bf16[96,14336]{1,0:T(8,128)(2,1)}, f32[1,3,128,128]{3,2,1,0:T(8,128)}) custom-call(s32[1,48]{1,0:T(1,128)} %ids_ref.3, s32[1,48]{1,0:T(1,128)} %get-tuple-element.6.other_ref, bf16[2,2,2,4,3,96,128]{6,5,4,3,2,1,0:T(8,128)(2,1)} %get-tuple-element.7.con_hbm, f32[1,3,128,128]{3,2,1,0:T(8,128)} %get-tuple-element.8.wgrad_in, ...), custom_call_target="tpu_custom_call" | custom-call | tf_op jit(solution)/shard_map/pallas_call | solution.py:493
